TPU v7x, 128 devices: a whole 4x4x4 slice. The times are simulated.
128 devices in a mesh: dp: 16 (over z, x), seq: 8 (over y, core).
Axes of the slice: x: 4, y: 4, z: 4, core: 2. Of those that a mesh axis runs over, the one named last changes fastest.
Arguments:
- queries: bfloat16 [16384, 4096], P(('dp', 'seq')), may hold values from -6 to 6
- keys: bfloat16 [16384, 4096], P(('dp', 'seq')), may hold values from -6 to 6
- values: bfloat16 [16384, 4096], P(('dp', 'seq')), may hold values from -6 to 6
- grad_mixed: bfloat16 [16384, 4096], P(('dp', 'seq')), may hold values from -6 to 6
- doc_lengths: int32 [16, 8], replicated, may hold values from 1 to 512, 1024 in all within a row
- owner: int32 [16], replicated, may hold values from 0 to 15, each once
Outputs:
- mixed: bfloat16 [16384, 4096], P(('dp', 'seq'))
- grad_queries: bfloat16 [16384, 4096], P(('dp', 'seq'))
- grad_keys: bfloat16 [16384, 4096], P(('dp', 'seq'))
- grad_values: bfloat16 [16384, 4096], P(('dp', 'seq'))
Inputs may be any that keep to these rules, and one draw needn't show every extreme that they name: `doc_lengths`: each row holds positive lengths that sum to 1024, the largest exactly 512. `owner`: a permutation of the data groups.
All inputs are finite; a program needn't handle non-finite values.
Results may differ from a plain program's by a relative error of at most 0.012.
Values may be sent and summed in bfloat16 or wider, within the bound.
No kernel may reach another device: no remote copies, remote signals or barrier semaphores. Data moves between devices by JAX's collectives and lax.ppermute only.
A program may use at most 128 MiB of HBM per device.

v0:
```python
import functools

import jax
import jax.numpy as jnp
from jax import lax
from jax.experimental import pallas as pl
from jax.experimental.pallas import tpu as pltpu
from jax.sharding import PartitionSpec as P

HEAD_DIM = 128
LOG2E = 1.4426950408889634
SCALE = HEAD_DIM ** (-0.5)
ROWS = 256
CHIPS, CORES = 4, 2
PEERS = CHIPS * CORES
CHUNKS = 2
HP = 2
WIDTH = HP * HEAD_DIM
BLOCKS = PEERS * 128 // ROWS
DOCS = 8
FIRSTS = 2 + BLOCKS
PARTS = 3
KEPT = (BLOCKS, PARTS, ROWS, ROWS)
NT = (((1,), (1,)), ((), ()))
TN = (((0,), (0,)), ((), ()))
ANY = pl.BlockSpec(memory_space=pl.ANY)
MIB = 1024 * 1024
VMEM = 62 * MIB


def position():
    me = lax.axis_index("seq")
    return lax.div(me, CORES), lax.rem(me, CORES)


def chip(y, d):
    return lax.rem(y + d + CHIPS, CHIPS)


def column(y, c, k):
    return pl.multiple_of((y * CHUNKS + k) * CORES * WIDTH + c * WIDTH, WIDTH)


def turn(x, d):
    pairs = [(i, (i // CORES + d) % CHIPS * CORES + i % CORES) for i in range(PEERS)]
    return lax.ppermute(x, "seq", pairs)


def swap_cores(x):
    return lax.ppermute(x, "seq", [(i, i ^ 1) for i in range(PEERS)])


def turn_across(x, d):
    pairs = [(i, (i // CORES + d) % CHIPS * CORES + 1 - i % CORES) for i in range(PEERS)]
    return lax.ppermute(x, "seq", pairs)


def turn_direct(parts):
    own, sib = list(parts[:CHIPS]), list(parts[CHIPS:])
    sib[0] = turn_across(sib[0], 0)
    for d in (1, 3, 2):
        own[d], sib[d] = turn(own[d], d), turn_across(sib[d], d)
    return own, sib


def turn_all(xs):
    got = {d: turn(xs[d], d) for d in (1, 3, 2)}
    return [xs[0], got[1], got[2], got[3]]


TOKEN = jax.ShapeDtypeStruct((8, 128), jnp.float32)


def cost(microseconds):
    return pl.CostEstimate(
        flops=int(microseconds * 1.1e9), bytes_accessed=MIB // 16, transcendentals=0
    )


def run_two_stages(into_vmem, out_of):
    for x in into_vmem:
        x.start()
    for x, nexts in zip(into_vmem, out_of):
        x.wait()
        for z in nexts:
            z.start()
    for nexts in out_of:
        for z in nexts:
            z.wait()


def copy_kernel(plan, inputs, shapes, pieces, after):
    n, m = len(inputs), len(pieces)

    def kernel(*refs):
        pairs = plan(refs[:n], refs[n + len(after) : -3 - m])
        held, arrive, leave = refs[-2 - m : -2], refs[-2], refs[-1]
        assert len(pairs) == m
        run_two_stages(
            [pltpu.make_async_copy(a, held[i], arrive.at[i]) for i, (a, _) in enumerate(pairs)],
            [[pltpu.make_async_copy(held[i], b, leave.at[i])] for i, (_, b) in enumerate(pairs)],
        )

    *outs, token = pl.pallas_call(
        kernel,
        out_shape=[jax.ShapeDtypeStruct(x, jnp.bfloat16) for x in shapes] + [TOKEN],
        in_specs=[ANY] * (n + len(after)),
        out_specs=[ANY] * (len(shapes) + 1),
        scratch_shapes=[pltpu.VMEM(x, jnp.bfloat16) for x in pieces]
        + [pltpu.SemaphoreType.DMA((m,)), pltpu.SemaphoreType.DMA((m,))],
        compiler_params=pltpu.CompilerParams(vmem_limit_bytes=VMEM),
        cost_estimate=cost(0.05),
    )(*inputs, *after)
    return outs, [token]


def gate(xs, after):
    def kernel(*refs):
        pass

    return pl.pallas_call(
        kernel,
        out_shape=[jax.ShapeDtypeStruct(x.shape, x.dtype) for x in xs],
        in_specs=[ANY] * (len(xs) + len(after)),
        out_specs=[ANY] * len(xs),
        input_output_aliases={i: i for i in range(len(xs))},
        compiler_params=pltpu.CompilerParams(vmem_limit_bytes=VMEM),
        cost_estimate=cost(0.05),
    )(*xs, *after)


def pack(arrays, k, slabs, after):
    n, rows = len(arrays), arrays[0].shape[0]

    def plan(ins, outs):
        y, c = position()
        return [
            (
                ins[a].at[:, pl.ds(column(chip(y, d), 1 - c if sib else c, k), WIDTH)],
                outs[sib * CHIPS + d].at[a],
            )
            for d in (1, 3, 0, 2)
            for sib in range(CORES)
            for a in range(n)
        ] + [
            (ins[a].at[:, pl.ds(column(chip(y, d), 1 - c, k), WIDTH)], outs[PEERS].at[d, i])
            for d in range(CHIPS)
            for i, (a, k) in enumerate(slabs)
        ]

    shapes = [(n, rows, WIDTH)] * PEERS + [(CHIPS, len(slabs), rows, WIDTH)]
    pieces = [(rows, WIDTH)] * (PEERS * n + CHIPS * len(slabs))
    return copy_kernel(plan, arrays, shapes, pieces, after)


def merge_columns(arrays, swapped, slabs, after):
    rows, n = arrays[0].shape[0], len(slabs)

    def plan(ins, outs):
        y, c = position()
        pairs = []
        for d in (1, 3, 2, 0):
            for i, (a, k) in enumerate(slabs):
                src = ins[a].at[:, pl.ds(column(chip(y, d), c, k), WIDTH)]
                pairs.append((src, outs[d].at[0, i]))
            pairs.append((ins[-1].at[d], outs[d].at[1]))
        return pairs

    shapes = [(CORES, n, rows, WIDTH)] * CHIPS
    pieces = ([(rows, WIDTH)] * n + [(n, rows, WIDTH)]) * CHIPS
    return copy_kernel(plan, list(arrays) + [swapped], shapes, pieces, after)


def pick_other_core_rows(got, after):
    def plan(ins, outs):
        return [(ins[d].at[1], outs[0].at[d]) for d in range(CHIPS)]

    shape = got[0].shape[1:]
    return copy_kernel(plan, got, [(CHIPS,) + shape], [shape] * CHIPS, after)


def unpack(own, sib, into, k, after):
    flat = list(own) + list(sib)
    arrays = []
    for x, _ in flat:
        if not any(x is z for z in arrays):
            arrays.append(x)
    where = [next(i for i, z in enumerate(arrays) if z is x) for x, _ in flat]
    n, rows, width = arrays[0].shape[-3:]
    olds = [] if into is None else list(into)
    order = [i * CHIPS + d for d in (0, 1, 3, 2) for i in range(CORES)]

    def kernel(*refs):
        ins = refs[: len(arrays)]
        outs = refs[len(arrays) + len(olds) + len(after) : -4]
        held, arrive, leave = refs[-3:]
        y, c = position()
        into_vmem, out_of = [], []
        for i in order:
            core = 1 - c if i >= CHIPS else c
            col = column(chip(y, -(i % CHIPS)), core, k)
            src = ins[where[i]]
            if flat[i][1] is not None:
                src = src.at[flat[i][1]]
            into_vmem.append(pltpu.make_async_copy(src, held.at[i], arrive.at[i]))
            out_of.append([
                pltpu.make_async_copy(
                    held.at[i, a], outs[a].at[:, pl.ds(col, width)], leave.at[i * n + a]
                )
                for a in range(n)
            ])
        run_two_stages(into_vmem, out_of)

    *outs, token = pl.pallas_call(
        kernel,
        out_shape=[jax.ShapeDtypeStruct((rows, PEERS * CHUNKS * WIDTH), jnp.bfloat16)] * n
        + [TOKEN],
        in_specs=[ANY] * (len(arrays) + len(olds) + len(after)),
        out_specs=[ANY] * (n + 1),
        scratch_shapes=[
            pltpu.VMEM((PEERS, n, rows, width), jnp.bfloat16),
            pltpu.SemaphoreType.DMA((PEERS,)),
            pltpu.SemaphoreType.DMA((PEERS * n,)),
        ],
        compiler_params=pltpu.CompilerParams(vmem_limit_bytes=VMEM),
        input_output_aliases={len(arrays) + a: a for a in range(len(olds))},
        cost_estimate=cost(0.05),
    )(*arrays, *olds, *after)
    return outs, [token]


def pick(parts, sender, after):
    groups = parts[0].shape[0]
    n = len(parts)

    def kernel(sender_ref, *refs):
        ins, out, (held, arrive, leave) = refs[:n], refs[n + len(after)], refs[-3:]
        into_vmem, out_of = [], []
        for g in range(groups):
            for k in range(n):
                i = g * n + k
                into_vmem.append(
                    pltpu.make_async_copy(ins[k].at[sender_ref[g]], held.at[i], arrive.at[i])
                )
                out_of.append([pltpu.make_async_copy(held.at[i], out.at[g, k], leave.at[i])])
        run_two_stages(into_vmem, out_of)

    slots, token = pl.pallas_call(
        kernel,
        out_shape=[jax.ShapeDtypeStruct((groups, n) + parts[0].shape[1:], jnp.bfloat16), TOKEN],
        grid_spec=pltpu.PrefetchScalarGridSpec(
            num_scalar_prefetch=1,
            grid=(1,),
            in_specs=[ANY] * (n + len(after)),
            out_specs=[ANY, ANY],
            scratch_shapes=[
                pltpu.VMEM((groups * n,) + parts[0].shape[1:], jnp.bfloat16),
                pltpu.SemaphoreType.DMA((groups * n,)),
                pltpu.SemaphoreType.DMA((groups * n,)),
            ],
        ),
        compiler_params=pltpu.CompilerParams(vmem_limit_bytes=VMEM),
        cost_estimate=cost(0.05),
    )(sender, *parts, *after)
    return slots, [token]


def settle(landed, after):
    _, peers, chunks, small, lanes = landed.shape
    groups = 8
    heads = landed.shape[0] // groups
    x = landed.reshape(heads, groups, peers, chunks, small, lanes)
    half = groups // 2

    def kernel(x_ref, *refs):
        o_ref = refs[len(after)]
        for s in range(peers):
            for k in range(chunks):
                for h in range(heads):
                    chip_, core = divmod(s, CORES)
                    col = (((chip_ * chunks + k) * CORES + core) * heads + h) * lanes
                    o_ref[:, col : col + lanes] = x_ref[h, :, s, k].reshape(half * small, lanes)

    mixed, token = pl.pallas_call(
        kernel,
        out_shape=[
            jax.ShapeDtypeStruct((groups * small, peers * chunks * heads * lanes), jnp.bfloat16),
            TOKEN,
        ],
        grid=(2,),
        in_specs=[
            pl.BlockSpec((heads, half, peers, chunks, small, lanes), lambda i: (0, i, 0, 0, 0, 0))
        ]
        + [ANY] * len(after),
        out_specs=[
            pl.BlockSpec((half * small, peers * chunks * heads * lanes), lambda i: (i, 0)),
            ANY,
        ],
        compiler_params=pltpu.CompilerParams(vmem_limit_bytes=VMEM),
        cost_estimate=cost(0.05),
    )(x, *after)
    return mixed, [token]


def triangle(after):
    a = lax.broadcasted_iota(jnp.int32, (ROWS, ROWS), 0)
    b = lax.broadcasted_iota(jnp.int32, (ROWS, ROWS), 1)
    return jnp.where((a > b) if after else (a < b), 1.0, 0.0).astype(jnp.bfloat16)


def gather_rows(pieces, scratch, scalars_ref):
    y, c = scalars_ref[0], scalars_ref[1]
    for i, ref in enumerate(pieces):
        p = chip(y, -(i % CHIPS)) * CORES + (1 - c if i >= CHIPS else c)
        x = ref[...]
        scratch[:, pl.ds(p, 1)] = x.reshape((scratch.shape[0], 1) + scratch.shape[2:])


def rows_of(ref, a, first, count, h):
    x = ref[a, pl.ds(first // 128, count // 128), :, h * HEAD_DIM : (h + 1) * HEAD_DIM]
    return x.reshape(count, HEAD_DIM)


def forward_kernel(scalars_ref, *refs):
    pieces = refs[:PEERS]
    out_ref, w_ref, sig_ref, _, tri_ref, acc_ref, qkv_ref = refs[-7:]
    heads = range(HP)
    i = pl.program_id(0)
    r0 = pl.multiple_of(i * ROWS, ROWS)

    @pl.when(i == 0)
    def _():
        tri_ref[...] = triangle(True)
        gather_rows(pieces, qkv_ref, scalars_ref)

    row = lax.broadcasted_iota(jnp.int32, (ROWS, 1), 0) + r0
    start = jnp.zeros((ROWS, 1), jnp.int32)
    for d in range(DOCS):
        first = scalars_ref[FIRSTS + d]
        start = jnp.where(row >= first, jnp.maximum(start, first), start)
    q = [rows_of(qkv_ref, 0, r0, ROWS, h) for h in heads]
    acc_ref[...] = jnp.zeros_like(acc_ref)

    def body(j, rest):
        lo = pl.multiple_of(r0 - j * ROWS, ROWS)
        col = lax.broadcasted_iota(jnp.int32, (ROWS, ROWS), 1) + lo
        allowed = (col >= start) & (col < row)
        left = []
        for h in heads:
            k, v = rows_of(qkv_ref, 1, lo, ROWS, h), rows_of(qkv_ref, 2, lo, ROWS, h)
            t = lax.dot_general(q[h], k, NT, preferred_element_type=jnp.float32)
            t = jnp.where(allowed, t * (SCALE * LOG2E), -1e30)
            tail = jnp.log2(1.0 + jnp.exp2(-jnp.abs(t)))
            z = jnp.maximum(t, 0.0) + tail
            ls = jnp.minimum(t, 0.0) - tail
            after = jnp.dot(
                z.astype(jnp.bfloat16), tri_ref[...], preferred_element_type=jnp.float32
            ) + rest[h]
            left.append(after[:, :1] + z[:, :1])
            w = jnp.exp2(ls - after).astype(jnp.bfloat16)
            acc_ref[h] += jnp.dot(w, v, preferred_element_type=jnp.float32)
            w_ref[h, 0, j] = w
            sig_ref[h, 0, j] = jnp.exp2(ls).astype(jnp.bfloat16)
        return tuple(left)

    lax.fori_loop(0, scalars_ref[2 + i], body, (jnp.zeros((ROWS, 1), jnp.float32),) * HP)

    for h in heads:
        x = acc_ref[h].astype(jnp.bfloat16)
        for r in range(ROWS // 128):
            for g in range(8):
                at = r * 128 + g * 16
                out_ref[h * 8 + g, pl.ds(r0 // 128 + r, 1), 0] = x[at : at + 16].reshape(
                    1, 16, HEAD_DIM
                )


def backward_kernel(by_chip, scalars_ref, *refs):
    pieces, (w_ref, sig_ref) = refs[:PEERS], refs[PEERS : PEERS + 2]
    outs = refs[-7 - (CHIPS if by_chip else PEERS) : -7]
    tri_ref, qkv_ref, dq_ref, acc_ref, dk_acc, dv_acc = refs[-6:]
    heads = range(HP)
    block = pl.program_id(0)
    r0 = pl.multiple_of(block * ROWS, ROWS)

    @pl.when(block == 0)
    def _():
        tri_ref[...] = triangle(False)
        gather_rows(pieces, qkv_ref, scalars_ref)
        dk_acc[...] = jnp.zeros_like(dk_acc)
        dv_acc[...] = jnp.zeros_like(dv_acc)

    q = [rows_of(qkv_ref, 0, r0, ROWS, h) for h in heads]
    g = [rows_of(qkv_ref, 3, r0, ROWS, h) for h in heads]
    acc_ref[...] = jnp.zeros_like(acc_ref)
    chunks = scalars_ref[2 + block]

    def body(i, upto):
        j = chunks - 1 - i
        lo = pl.multiple_of(r0 - j * ROWS, ROWS)
        here = pl.ds(lo, ROWS)
        right = []
        for h in heads:
            k, v = rows_of(qkv_ref, 1, lo, ROWS, h), rows_of(qkv_ref, 2, lo, ROWS, h)
            w = w_ref[h, 0, j]
            dv_acc[h, here] += lax.dot_general(w, g[h], TN, preferred_element_type=jnp.float32)
            dw = lax.dot_general(g[h], v, NT, preferred_element_type=jnp.float32)
            a = w.astype(jnp.float32) * dw
            total = jnp.dot(
                a.astype(jnp.bfloat16), tri_ref[...], preferred_element_type=jnp.float32
            ) + (a + upto[h])
            right.append(total[:, ROWS - 1 :])
            ds = (a - sig_ref[h, 0, j].astype(jnp.float32) * total).astype(jnp.bfloat16)
            acc_ref[h] += jnp.dot(ds, k, preferred_element_type=jnp.float32)
            dk_acc[h, here] += lax.dot_general(ds, q[h], TN, preferred_element_type=jnp.float32)
        return tuple(right)

    lax.fori_loop(0, chunks, body, (jnp.zeros((ROWS, 1), jnp.float32),) * HP)
    for h in heads:
        dq_ref[h, pl.ds(r0, ROWS)] = (acc_ref[h] * SCALE).astype(jnp.bfloat16)

    @pl.when(pl.program_id(0) == BLOCKS - 1)
    def _():
        y, c = scalars_ref[0], scalars_ref[1]
        for i in range(PEERS):
            d, sib = i % CHIPS, i // CHIPS
            ref = outs[d].at[sib] if by_chip else outs[i]
            p = chip(y, d) * CORES + (1 - c if sib else c)
            at = pl.ds(pl.multiple_of(p * 128, 128), 128)
            for h in heads:
                cols = slice(h * HEAD_DIM, (h + 1) * HEAD_DIM)
                ref[0, :, cols] = dq_ref[h, at]
                ref[1, :, cols] = (dk_acc[h, at] * SCALE).astype(jnp.bfloat16)
                ref[2, :, cols] = dv_acc[h, at].astype(jnp.bfloat16)


def kept_spec():
    return pl.BlockSpec((HP, 1) + KEPT[1:], lambda i, u: (0, i, 0, 0, 0))


def whole(shape):
    return pl.BlockSpec(shape, lambda i, u: (0,) * len(shape))


def forward(pieces, scalars, shared, k, after):
    kept = jax.ShapeDtypeStruct((HP,) + KEPT, jnp.bfloat16)
    out = (HP * 8, PEERS, CHUNKS, 16, HEAD_DIM)
    out_spec = pl.BlockSpec((HP * 8, PEERS, 1, 16, HEAD_DIM), lambda i, u: (0, 0, k, 0, 0))
    olds = [] if shared is None else [shared]
    out, *saved, token = pl.pallas_call(
        forward_kernel,
        out_shape=[jax.ShapeDtypeStruct(out, jnp.bfloat16), kept, kept, TOKEN],
        grid_spec=pltpu.PrefetchScalarGridSpec(
            num_scalar_prefetch=1,
            grid=(BLOCKS,),
            in_specs=[spec for _, spec in pieces] + [ANY] * (len(olds) + len(after)),
            out_specs=[out_spec, kept_spec(), kept_spec(), ANY],
            scratch_shapes=[
                pltpu.VMEM((ROWS, ROWS), jnp.bfloat16),
                pltpu.VMEM((HP, ROWS, HEAD_DIM), jnp.float32),
                pltpu.VMEM((3, PEERS, 128, WIDTH), jnp.bfloat16),
            ],
        ),
        compiler_params=pltpu.CompilerParams(vmem_limit_bytes=VMEM),
        input_output_aliases={1 + PEERS: 0} if olds else {},
        cost_estimate=cost(10 if k else 0.05),
    )(scalars, *[x for x, _ in pieces], *olds, *after)
    return out, saved, [token]


def backward(pieces, saved, scalars, by_chip, after):
    count = PEERS * 128
    outs = [(CORES, 3, 128, WIDTH)] * CHIPS if by_chip else [(3, 128, WIDTH)] * PEERS
    *grads, token = pl.pallas_call(
        functools.partial(backward_kernel, by_chip),
        out_shape=[jax.ShapeDtypeStruct(x, jnp.bfloat16) for x in outs] + [TOKEN],
        grid_spec=pltpu.PrefetchScalarGridSpec(
            num_scalar_prefetch=1,
            grid=(BLOCKS,),
            in_specs=[spec for _, spec in pieces]
            + [kept_spec(), kept_spec()]
            + [ANY] * len(after),
            out_specs=[whole(x) for x in outs] + [ANY],
            scratch_shapes=[
                pltpu.VMEM((ROWS, ROWS), jnp.bfloat16),
                pltpu.VMEM((4, PEERS, 128, WIDTH), jnp.bfloat16),
                pltpu.VMEM((HP, count, HEAD_DIM), jnp.bfloat16),
                pltpu.VMEM((HP, ROWS, HEAD_DIM), jnp.float32),
                pltpu.VMEM((HP, count, HEAD_DIM), jnp.float32),
                pltpu.VMEM((HP, count, HEAD_DIM), jnp.float32),
            ],
        ),
        compiler_params=pltpu.CompilerParams(vmem_limit_bytes=VMEM),
        cost_estimate=cost(15),
    )(scalars, *[x for x, _ in pieces], *saved, *after)
    return grads, [token]


def at_slabs(x, index, first, count):
    shape = (1, count) + x.shape[2:]
    return x, pl.BlockSpec(shape, lambda i, u: (index, first // count, 0, 0))


def at_first(x, first, count):
    return x, pl.BlockSpec((count,) + x.shape[1:], lambda i, u: (first // count, 0, 0))


def document_scalars(lengths, count):
    firsts = jnp.cumsum(lengths) - lengths
    places = jnp.arange(0, count, ROWS, dtype=jnp.int32)
    start = jnp.max(jnp.where(firsts[None, :] <= places[:, None], firsts[None, :], 0), axis=1)
    chunks = jnp.clip(places // ROWS - start // ROWS + 1, 1, jnp.minimum(places // ROWS + 1, PARTS))
    return jnp.concatenate([chunks, firsts]).astype(jnp.int32)


def local(queries, keys, values, grad_mixed, doc_lengths, owner):
    rows, width = queries.shape
    group = lax.axis_index("dp")
    groups = lax.axis_size("dp")

    lengths = lax.dynamic_index_in_dim(doc_lengths, group, 0, keepdims=False)
    y, c = position()
    scalars = jnp.concatenate(
        [jnp.stack([y, c]).astype(jnp.int32), document_scalars(lengths, rows * PEERS)]
    )
    ids = jnp.arange(groups, dtype=jnp.int32)
    sender = jnp.sum(jnp.where(owner[None, :] == ids[:, None], ids[None, :], 0), axis=1)
    sender = jnp.clip(sender, 0, groups - 1)

    inputs = [queries, keys, values, grad_mixed]

    slabs = [(a, 1) for a in range(4)]
    (*parts, other), token = pack(inputs, 0, slabs, [])
    own, sib = turn_direct(parts)
    second, token = merge_columns(inputs, swap_cores(other), slabs, token)
    second = turn_all(second)

    pieces = [at_first(x, 0, 3) for x in own + sib]
    out, saved, token = forward(pieces, scalars, None, 0, token)
    pieces = [at_first(x, 0, 4) for x in own + sib]
    got, token = backward(pieces, saved, scalars, True, token)
    got = turn_all(got)

    pieces = [at_slabs(x, core, 0, 3) for core in range(CORES) for x in second]
    out, saved, token = forward(pieces, scalars, out, 1, token)
    spread = lax.all_to_all(
        out.reshape(groups * PEERS * CHUNKS, 16, HEAD_DIM),
        ("dp", "seq"), split_axis=0, concat_axis=0, tiled=True,
    )
    pieces = [at_slabs(x, core, 0, 4) for core in range(CORES) for x in second]
    parts, token = backward(pieces, saved, scalars, False, token)
    parts = gate(parts, token + got[1:])
    own, sib = turn_direct(parts)

    slots, token = pick([spread.reshape(groups, PEERS * CHUNKS, 16, HEAD_DIM)], sender, token)
    landed = lax.all_to_all(slots, "dp", split_axis=0, concat_axis=0, tiled=True)
    landed = landed.reshape(groups, PEERS, CHUNKS, 16, HEAD_DIM)

    near = [own[1], sib[1], own[3], sib[3]]
    (other,), token = pick_other_core_rows(got, token + near)
    other = swap_cores(other)
    grads, token = unpack(
        [(x, 0) for x in got], [(other, d) for d in range(CHIPS)], None, 0, token
    )
    grads, token = unpack([(x, None) for x in own], [(x, None) for x in sib], grads, 1, token)
    mixed, token = settle(landed, token)
    return (mixed, grads[0], grads[1], grads[2])


def solution(mesh):
    placed = P(("dp", "seq"), None)
    return jax.shard_map(
        local,
        mesh=mesh,
        in_specs=(placed,) * 4 + (P(), P()),
        out_specs=(placed,) * 4,
        check_vma=False,
    )
```

profile of v0, /device:TPU:1, one launch (start us, length us, event | category | flops | bytes accessed | tf_op | source)
XLA Modules:
  0.0 141.0 jit_solution(8718615956537389572)
XLA Ops:
  0.7 4.0 %shard_map.93 = (bf16[4,128,256]{2,1,0:T(8,128)(2,1)}, bf16[4,128,256]{2,1,0:T(8,128)(2,1)}, bf16[4,128,256]{2,1,0:T(8,128)(2,1)}, bf16[4,128,256]{2,1,0:T(8,128...) custom-call(bf16[128,4096]{1,0:T(8,128)(2,1)} %refs_0_.3, ...), custom_call_target="tpu_custom_call" | custom-call | flops 55000000 | bytes 65536 | tf_op jit(solution)/shard_map/pallas_call | solution.py:104
  6.1 2.8 %collective-permute-start.10 = (bf16[4,128,256]{2,1,0:T(8,128)(2,1)}, bf16[4,128,256]{2,1,0:T(8,128)(2,1)S(1)}, u32[]{:S(2)}, u32[]{:S(2)}) collective-permute-start(bf16[4,128,256]{2,1,0:T(8,128)(2,1)} %get-tuple-element.75), channel_id=1, source_target_pairs={{0,7},{1,6},{2,1},{3,0},{4,3},{5,2},{6,5},{7,4},{8,15},{9,14},{10,... | collective-permute-start | bytes 786440 | tf_op jit(solution)/shard_map/ppermute | solution.py:55
  8.9 1.6 %collective-permute-start.5 = (bf16[4,128,256]{2,1,0:T(8,128)(2,1)}, bf16[4,128,256]{2,1,0:T(8,128)(2,1)S(1)}, u32[]{:S(2)}, u32[]{:S(2)}) collective-permute-start(bf16[4,128,256]{2,1,0:T(8,128)(2,1)} %get-tuple-element.70), channel_id=1, source_target_pairs={{0,4},{1,5},{2,6},{3,7},{4,0},{5,1},{6,2},{7,3},{8,12},{9,13},{10,... | collective-permute-start | bytes 786440 | tf_op jit(solution)/shard_map/ppermute | solution.py:46
  12.1 8.1 %collective-permute-done.10.refs_7_ = bf16[4,128,256]{2,1,0:T(8,128)(2,1)S(1)} collective-permute-done((bf16[4,128,256]{2,1,0:T(8,128)(2,1)}, bf16[4,128,256]{2,1,0:T(8,128)(2,1)S(1)}, u32[]{:S(2)}, u32[]{:S(2)}) %collective-permute-start.10) | collective-permute-done | bytes 262176 | tf_op jit(solution)/shard_map/ppermute | solution.py:55
  20.3 1.7 %collective-permute-start.7 = (bf16[4,128,256]{2,1,0:T(8,128)(2,1)}, bf16[4,128,256]{2,1,0:T(8,128)(2,1)}, u32[]{:S(2)}, u32[]{:S(2)}) collective-permute-start(bf16[4,128,256]{2,1,0:T(8,128)(2,1)} %get-tuple-element.72), channel_id=1, source_target_pairs={{0,1},{1,0},{2,3},{3,2},{4,5},{5,4},{6,7},{7,6},{8,9},{9,8},{10,11... | collective-permute-start | bytes 786440 | tf_op jit(solution)/shard_map/ppermute | solution.py:55
  23.4 2.7 %collective-permute-start.9 = (bf16[4,128,256]{2,1,0:T(8,128)(2,1)}, bf16[4,128,256]{2,1,0:T(8,128)(2,1)}, u32[]{:S(2)}, u32[]{:S(2)}) collective-permute-start(bf16[4,128,256]{2,1,0:T(8,128)(2,1)} %get-tuple-element.74), channel_id=1, source_target_pairs={{0,5},{1,4},{2,7},{3,6},{4,1},{5,0},{6,3},{7,2},{8,13},{9,12},{10,... | collective-permute-start | bytes 786440 | tf_op jit(solution)/shard_map/ppermute | solution.py:55
  26.9 2.7 %shard_map.94 = (bf16[2,4,128,256]{3,2,1,0:T(8,128)(2,1)}, bf16[2,4,128,256]{3,2,1,0:T(8,128)(2,1)}, bf16[2,4,128,256]{3,2,1,0:T(8,128)(2,1)}, bf16[2,4,128,256]{3,2,1,0:T(8,128)(2,1)}, f32[8,128]{1,0:T(8,128)}) custom-call(bf16[128,4096]{1,0:T(8,128)(2,1)} %refs_0_.3, bf16[128,4096]{1,0:T(8,128)(2,1)} %refs_1_.3, bf16[128,4096]{1,0:T(8,128)(2,1)} %refs_2_.3, ...), custom_call_target="tpu_custom_call" | custom-call | flops 55000000 | bytes 65536 | tf_op jit(solution)/shard_map/pallas_call | solution.py:104
  30.5 1.7 %collective-permute-start.2 = (bf16[2,4,128,256]{3,2,1,0:T(8,128)(2,1)}, bf16[2,4,128,256]{3,2,1,0:T(8,128)(2,1)S(1)}, u32[]{:S(2)}, u32[]{:S(2)}) collective-permute-start(bf16[2,4,128,256]{3,2,1,0:T(8,128)(2,1)} %get-tuple-element.66), channel_id=1, source_target_pairs={{0,4},{1,5},{2,6},{3,7},{4,0},{5,1},{6,2},{7,3},{8,12},{9,13},{10,... | collective-permute-start | bytes 1572872 | tf_op jit(solution)/shard_map/ppermute | solution.py:46
  33.5 5.4 %collective-permute-done.9.refs_6_ = bf16[4,128,256]{2,1,0:T(8,128)(2,1)} collective-permute-done((bf16[4,128,256]{2,1,0:T(8,128)(2,1)}, bf16[4,128,256]{2,1,0:T(8,128)(2,1)}, u32[]{:S(2)}, u32[]{:S(2)}) %collective-permute-start.9) | collective-permute-done | bytes 262176 | tf_op jit(solution)/shard_map/ppermute | solution.py:55
  39.0 10.8 %shard_map.95 = (bf16[16,8,2,16,128]{4,3,2,1,0:T(8,128)(2,1)}, bf16[2,4,3,256,256]{4,3,2,1,0:T(8,128)(2,1)}, bf16[2,4,3,256,256]{4,3,2,1,0:T(8,128)(2,1)}, f32[8,128]{1,0:T(8,128)}) custom-call(s32[14]{0:T(128)} %pad_add_fusion.scalars_ref, bf16[4,128,256]{2,1,0:T(8,128)(2,1)} %get-tuple-element.68.refs_0_, bf16[4,128,256]{2,1,0:T(8,128)(2,1)} %copy-done.8, ...), custom_call_target="tpu_custom_call" | custom-call | flops 55000000 | bytes 65536 | tf_op jit(solution)/shard_map/pallas_call | solution.py:450
  49.7 13.0 %shard_map.96 = (bf16[2,3,128,256]{3,2,1,0:T(8,128)(2,1)}, bf16[2,3,128,256]{3,2,1,0:T(8,128)(2,1)}, bf16[2,3,128,256]{3,2,1,0:T(8,128)(2,1)}, bf16[2,3,128,256]{3,2,1,0:T(8,128)(2,1)}, f32[8,128]{1,0:T(8,128)}) custom-call(s32[14]{0:T(128)} %pad_add_fusion.scalars_ref, bf16[4,128,256]{2,1,0:T(8,128)(2,1)} %get-tuple-element.68.refs_0_, ...), custom_call_target="tpu_custom_call" | custom-call | flops 16499999744 | bytes 65536 | tf_op jit(solution)/shard_map/pallas_call | solution.py:474
  64.3 2.0 %collective-permute-start.13 = (bf16[2,3,128,256]{3,2,1,0:T(8,128)(2,1)}, bf16[2,3,128,256]{3,2,1,0:T(8,128)(2,1)}, u32[]{:S(2)}, u32[]{:S(2)}) collective-permute-start(bf16[2,3,128,256]{3,2,1,0:T(8,128)(2,1)} %get-tuple-element.98), channel_id=1, source_target_pairs={{0,6},{1,7},{2,0},{3,1},{4,2},{5,3},{6,4},{7,5},{8,14},{9,15},{10,... | collective-permute-start | bytes 1179656 | tf_op jit(solution)/shard_map/ppermute | solution.py:46
  67.1 10.8 %shard_map.97 = (bf16[16,8,2,16,128]{4,3,2,1,0:T(8,128)(2,1)}, bf16[2,4,3,256,256]{4,3,2,1,0:T(8,128)(2,1)}, bf16[2,4,3,256,256]{4,3,2,1,0:T(8,128)(2,1)}, f32[8,128]{1,0:T(8,128)}) custom-call(s32[14]{0:T(128)} %pad_add_fusion.scalars_ref, bf16[2,4,128,256]{3,2,1,0:T(8,128)(2,1)} %get-tuple-element.64.refs_0_.refs_4_, ...), custom_call_target="tpu_custom_call", output_to_operand_aliasing={{0}: (9, {})} | custom-call | flops 11000000512 | bytes 65536 | tf_op jit(solution)/shard_map/pallas_call | solution.py:450
  77.9 10.6 %all-to-all-start = ((bf16[256,16,128]{2,1,0:T(8,128)(2,1)}), bf16[256,16,128]{2,1,0:T(8,128)(2,1)S(1)}, u32[]{:S(2)}, u32[]{:S(2)}) async-start(bf16[256,16,128]{2,1,0:T(8,128)(2,1)} %bitcast.18), calls=%async_computation | async-start | bytes 2097152 | tf_op jit(solution)/shard_map/all_to_all | solution.py:546
  88.5 13.0 %shard_map.98 = (bf16[3,128,256]{2,1,0:T(8,128)(2,1)}, bf16[3,128,256]{2,1,0:T(8,128)(2,1)}, bf16[3,128,256]{2,1,0:T(8,128)(2,1)}, bf16[3,128,256]{2,1,0:T(8,128...) custom-call(s32[14]{0:T(128)} %pad_add_fusion.scalars_ref, ...), custom_call_target="tpu_custom_call" | custom-call | flops 16499999744 | bytes 65536 | tf_op jit(solution)/shard_map/pallas_call | solution.py:474
  106.0 2.0 %collective-permute-start.20 = (bf16[3,128,256]{2,1,0:T(8,128)(2,1)}, bf16[3,128,256]{2,1,0:T(8,128)(2,1)}, u32[]{:S(2)}, u32[]{:S(2)}) collective-permute-start(bf16[3,128,256]{2,1,0:T(8,128)(2,1)} %get-tuple-element.106), channel_id=1, source_target_pairs={{0,7},{1,6},{2,1},{3,0},{4,3},{5,2},{6,5},{7,4},{8,15},{9,14},{10,... | collective-permute-start | bytes 589832 | tf_op jit(solution)/shard_map/ppermute | solution.py:55
  109.5 2.9 %shard_map.99 = (bf16[16,1,16,16,128]{4,3,2,1,0:T(8,128)(2,1)}, f32[8,128]{1,0:T(8,128)}) custom-call(s32[16]{0:T(128)} %broadcast_clamp_fusion.sender_ref, bf16[16,16,16,128]{3,2,1,0:T(8,128)(2,1)} %bitcast.17, f32[8,128]{1,0:T(8,128)} %get-tuple-element.86.refs_1_.refs_8_), custom_call_target="tpu_custom_call" | custom-call | flops 55000000 | bytes 65536 | tf_op jit(solution)/shard_map/pallas_call | solution.py:248
  112.4 7.1 %all-to-all-start.1 = ((bf16[16,1,16,16,128]{4,3,2,1,0:T(8,128)(2,1)}), bf16[16,1,16,16,128]{4,3,2,1,0:T(8,128)(2,1)S(1)}, u32[]{:S(2)}, u32[]{:S(2)}) async-start(bf16[16,1,16,16,128]{4,3,2,1,0:T(8,128)(2,1)} %get-tuple-element.87), calls=%async_computation.1 | async-start | bytes 2097152 | tf_op jit(solution)/shard_map/all_to_all | solution.py:556
  119.5 2.0 %shard_map.101 = (bf16[4,3,128,256]{3,2,1,0:T(8,128)(2,1)}, f32[8,128]{1,0:T(8,128)}) custom-call(bf16[2,3,128,256]{3,2,1,0:T(8,128)(2,1)} %get-tuple-element.107.refs_0_, bf16[2,3,128,256]{3,2,1,0:T(8,128)(2,1)} %copy-done.3, bf16[2,3,128,256]{3,2,1,0:T(8,128)(2,1)} %copy-done.4, bf16[2,3,128,256]{3,2,1,0:T(8,128)(2,1)} %collective-permute-done.13.refs_11_.refs_3_, ...), custom_call_target="tpu_custom_call" | custom-call | flops 55000000 | bytes 65536 | tf_op jit(solution)/shard_map/pallas_call | solution.py:104
  123.6 2.6 %collective-permute-start.19 = (bf16[3,128,256]{2,1,0:T(8,128)(2,1)}, bf16[3,128,256]{2,1,0:T(8,128)(2,1)}, u32[]{:S(2)}, u32[]{:S(2)}) collective-permute-start(bf16[3,128,256]{2,1,0:T(8,128)(2,1)} %get-tuple-element.105), channel_id=1, source_target_pairs={{0,5},{1,4},{2,7},{3,6},{4,1},{5,0},{6,3},{7,2},{8,13},{9,12},{10,... | collective-permute-start | bytes 589832 | tf_op jit(solution)/shard_map/ppermute | solution.py:55
  127.1 2.4 %shard_map.102 = (bf16[128,4096]{1,0:T(8,128)(2,1)}, bf16[128,4096]{1,0:T(8,128)(2,1)}, bf16[128,4096]{1,0:T(8,128)(2,1)}, f32[8,128]{1,0:T(8,128)}) custom-call(bf16[2,3,128,256]{3,2,1,0:T(8,128)(2,1)} %get-tuple-element.107.refs_0_, bf16[2,3,128,256]{3,2,1,0:T(8,128)(2,1)} %copy-done.3, bf16[2,3,128,256]{3,2,1,0:T(8,128)(2,1)} %copy-done.4, ...), custom_call_target="tpu_custom_call" | custom-call | flops 55000000 | bytes 65536 | tf_op jit(solution)/shard_map/pallas_call | solution.py:214
  131.1 4.4 %collective-permute-done.19.refs_6_ = bf16[3,128,256]{2,1,0:T(8,128)(2,1)} collective-permute-done((bf16[3,128,256]{2,1,0:T(8,128)(2,1)}, bf16[3,128,256]{2,1,0:T(8,128)(2,1)}, u32[]{:S(2)}, u32[]{:S(2)}) %collective-permute-start.19) | collective-permute-done | bytes 196640 | tf_op jit(solution)/shard_map/ppermute | solution.py:55
  135.5 2.4 %shard_map.103 = (bf16[128,4096]{1,0:T(8,128)(2,1)}, bf16[128,4096]{1,0:T(8,128)(2,1)}, bf16[128,4096]{1,0:T(8,128)(2,1)}, f32[8,128]{1,0:T(8,128)}) custom-call(bf16[3,128,256]{2,1,0:T(8,128)(2,1)} %get-tuple-element.99.refs_0_, ...), custom_call_target="tpu_custom_call", output_to_operand_aliasing={{0}: (8, {}), {1}: (9, {}), {2}: (10, {})} | custom-call | flops 55000000 | bytes 65536 | tf_op jit(solution)/shard_map/pallas_call | solution.py:214
  138.9 2.1 %shard_map.104 = (bf16[128,4096]{1,0:T(8,128)(2,1)}, f32[8,128]{1,0:T(8,128)}) custom-call(bf16[2,8,8,2,16,128]{5,4,3,2,1,0:T(8,128)(2,1)} %bitcast.16, f32[8,128]{1,0:T(8,128)} %get-tuple-element.115.refs_0_), custom_call_target="tpu_custom_call" | custom-call | flops 55000000 | bytes 65536 | tf_op jit(solution)/shard_map/pallas_call | solution.py:284
  (73 shorter events, 21.4 us)
Async XLA Ops:
  4.6 18.8 %collective-permute-start = (bf16[4,4,128,256]{3,2,1,0:T(8,128)(2,1)}, bf16[4,4,128,256]{3,2,1,0:T(8,128)(2,1)S(1)}, u32[]{:S(2)}, u32[]{:S(2)}) collective-permute-start(bf16[4,4,128,256]{3,2,1,0:T(8,128)(2,1)} %get-tuple-element.62), channel_id=1, source_target_pairs={{0,1},{1,0},{2,3},{3,2},{4,5},{5,4},{6,7},{7,6},{8,9},{9,8},{10,11... | collective-permute-start | bytes 3145736 | tf_op jit(solution)/shard_map/ppermute | solution.py:50
  6.1 14.1 %collective-permute-start.10 = (bf16[4,128,256]{2,1,0:T(8,128)(2,1)}, bf16[4,128,256]{2,1,0:T(8,128)(2,1)S(1)}, u32[]{:S(2)}, u32[]{:S(2)}) collective-permute-start(bf16[4,128,256]{2,1,0:T(8,128)(2,1)} %get-tuple-element.75), channel_id=1, source_target_pairs={{0,7},{1,6},{2,1},{3,0},{4,3},{5,2},{6,5},{7,4},{8,15},{9,14},{10,... | collective-permute-start | bytes 786440 | tf_op jit(solution)/shard_map/ppermute | solution.py:55
  8.9 14.5 %collective-permute-start.4 = (bf16[4,128,256]{2,1,0:T(8,128)(2,1)}, bf16[4,128,256]{2,1,0:T(8,128)(2,1)S(1)}, u32[]{:S(2)}, u32[]{:S(2)}) collective-permute-start(bf16[4,128,256]{2,1,0:T(8,128)(2,1)} %get-tuple-element.69), channel_id=1, source_target_pairs={{0,2},{1,3},{2,4},{3,5},{4,6},{5,7},{6,0},{7,1},{8,10},{9,11},{10,... | collective-permute-start | bytes 786440 | tf_op jit(solution)/shard_map/ppermute | solution.py:46
  8.9 20.6 %collective-permute-start.5 = (bf16[4,128,256]{2,1,0:T(8,128)(2,1)}, bf16[4,128,256]{2,1,0:T(8,128)(2,1)S(1)}, u32[]{:S(2)}, u32[]{:S(2)}) collective-permute-start(bf16[4,128,256]{2,1,0:T(8,128)(2,1)} %get-tuple-element.70), channel_id=1, source_target_pairs={{0,4},{1,5},{2,6},{3,7},{4,0},{5,1},{6,2},{7,3},{8,12},{9,13},{10,... | collective-permute-start | bytes 786440 | tf_op jit(solution)/shard_map/ppermute | solution.py:46
  10.6 19.9 %collective-permute-start.6 = (bf16[4,128,256]{2,1,0:T(8,128)(2,1)}, bf16[4,128,256]{2,1,0:T(8,128)(2,1)}, u32[]{:S(2)}, u32[]{:S(2)}) collective-permute-start(bf16[4,128,256]{2,1,0:T(8,128)(2,1)} %get-tuple-element.71), channel_id=1, source_target_pairs={{0,6},{1,7},{2,0},{3,1},{4,2},{5,3},{6,4},{7,5},{8,14},{9,15},{10,... | collective-permute-start | bytes 786440 | tf_op jit(solution)/shard_map/ppermute | solution.py:46
  20.3 11.9 %collective-permute-start.7 = (bf16[4,128,256]{2,1,0:T(8,128)(2,1)}, bf16[4,128,256]{2,1,0:T(8,128)(2,1)}, u32[]{:S(2)}, u32[]{:S(2)}) collective-permute-start(bf16[4,128,256]{2,1,0:T(8,128)(2,1)} %get-tuple-element.72), channel_id=1, source_target_pairs={{0,1},{1,0},{2,3},{3,2},{4,5},{5,4},{6,7},{7,6},{8,9},{9,8},{10,11... | collective-permute-start | bytes 786440 | tf_op jit(solution)/shard_map/ppermute | solution.py:55
  23.4 10.1 %collective-permute-start.8 = (bf16[4,128,256]{2,1,0:T(8,128)(2,1)}, bf16[4,128,256]{2,1,0:T(8,128)(2,1)}, u32[]{:S(2)}, u32[]{:S(2)}) collective-permute-start(bf16[4,128,256]{2,1,0:T(8,128)(2,1)} %get-tuple-element.73), channel_id=1, source_target_pairs={{0,3},{1,2},{2,5},{3,4},{4,7},{5,6},{6,1},{7,0},{8,11},{9,10},{10,... | collective-permute-start | bytes 786440 | tf_op jit(solution)/shard_map/ppermute | solution.py:55
  23.4 15.5 %collective-permute-start.9 = (bf16[4,128,256]{2,1,0:T(8,128)(2,1)}, bf16[4,128,256]{2,1,0:T(8,128)(2,1)}, u32[]{:S(2)}, u32[]{:S(2)}) collective-permute-start(bf16[4,128,256]{2,1,0:T(8,128)(2,1)} %get-tuple-element.74), channel_id=1, source_target_pairs={{0,5},{1,4},{2,7},{3,6},{4,1},{5,0},{6,3},{7,2},{8,13},{9,12},{10,... | collective-permute-start | bytes 786440 | tf_op jit(solution)/shard_map/ppermute | solution.py:55
  29.6 34.7 %collective-permute-start.1 = (bf16[2,4,128,256]{3,2,1,0:T(8,128)(2,1)}, bf16[2,4,128,256]{3,2,1,0:T(8,128)(2,1)S(1)}, u32[]{:S(2)}, u32[]{:S(2)}) collective-permute-start(bf16[2,4,128,256]{3,2,1,0:T(8,128)(2,1)} %get-tuple-element.65), channel_id=1, source_target_pairs={{0,2},{1,3},{2,4},{3,5},{4,6},{5,7},{6,0},{7,1},{8,10},{9,11},{10,... | collective-permute-start | bytes 1572872 | tf_op jit(solution)/shard_map/ppermute | solution.py:46
  30.5 35.8 %collective-permute-start.2 = (bf16[2,4,128,256]{3,2,1,0:T(8,128)(2,1)}, bf16[2,4,128,256]{3,2,1,0:T(8,128)(2,1)S(1)}, u32[]{:S(2)}, u32[]{:S(2)}) collective-permute-start(bf16[2,4,128,256]{3,2,1,0:T(8,128)(2,1)} %get-tuple-element.66), channel_id=1, source_target_pairs={{0,4},{1,5},{2,6},{3,7},{4,0},{5,1},{6,2},{7,3},{8,12},{9,13},{10,... | collective-permute-start | bytes 1572872 | tf_op jit(solution)/shard_map/ppermute | solution.py:46
  32.2 34.1 %collective-permute-start.3 = (bf16[2,4,128,256]{3,2,1,0:T(8,128)(2,1)}, bf16[2,4,128,256]{3,2,1,0:T(8,128)(2,1)}, u32[]{:S(2)}, u32[]{:S(2)}) collective-permute-start(bf16[2,4,128,256]{3,2,1,0:T(8,128)(2,1)} %get-tuple-element.67), channel_id=1, source_target_pairs={{0,6},{1,7},{2,0},{3,1},{4,2},{5,3},{6,4},{7,5},{8,14},{9,15},{10,... | collective-permute-start | bytes 1572872 | tf_op jit(solution)/shard_map/ppermute | solution.py:46
  62.7 38.8 %collective-permute-start.11 = (bf16[2,3,128,256]{3,2,1,0:T(8,128)(2,1)}, bf16[2,3,128,256]{3,2,1,0:T(8,128)(2,1)S(1)}, u32[]{:S(2)}, u32[]{:S(2)}) collective-permute-start(bf16[2,3,128,256]{3,2,1,0:T(8,128)(2,1)} %get-tuple-element.96), channel_id=1, source_target_pairs={{0,2},{1,3},{2,4},{3,5},{4,6},{5,7},{6,0},{7,1},{8,10},{9,11},{10,... | collective-permute-start | bytes 1179656 | tf_op jit(solution)/shard_map/ppermute | solution.py:46
  62.7 38.8 %collective-permute-start.12 = (bf16[2,3,128,256]{3,2,1,0:T(8,128)(2,1)}, bf16[2,3,128,256]{3,2,1,0:T(8,128)(2,1)S(1)}, u32[]{:S(2)}, u32[]{:S(2)}) collective-permute-start(bf16[2,3,128,256]{3,2,1,0:T(8,128)(2,1)} %get-tuple-element.97), channel_id=1, source_target_pairs={{0,4},{1,5},{2,6},{3,7},{4,0},{5,1},{6,2},{7,3},{8,12},{9,13},{10,... | collective-permute-start | bytes 1179656 | tf_op jit(solution)/shard_map/ppermute | solution.py:46
  64.3 37.2 %collective-permute-start.13 = (bf16[2,3,128,256]{3,2,1,0:T(8,128)(2,1)}, bf16[2,3,128,256]{3,2,1,0:T(8,128)(2,1)}, u32[]{:S(2)}, u32[]{:S(2)}) collective-permute-start(bf16[2,3,128,256]{3,2,1,0:T(8,128)(2,1)} %get-tuple-element.98), channel_id=1, source_target_pairs={{0,6},{1,7},{2,0},{3,1},{4,2},{5,3},{6,4},{7,5},{8,14},{9,15},{10,... | collective-permute-start | bytes 1179656 | tf_op jit(solution)/shard_map/ppermute | solution.py:46
  77.9 30.7 %all-to-all-start = ((bf16[256,16,128]{2,1,0:T(8,128)(2,1)}), bf16[256,16,128]{2,1,0:T(8,128)(2,1)S(1)}, u32[]{:S(2)}, u32[]{:S(2)}) async-start(bf16[256,16,128]{2,1,0:T(8,128)(2,1)} %bitcast.18), calls=%async_computation | async-start | bytes 2097152 | tf_op jit(solution)/shard_map/all_to_all | solution.py:546
  102.4 17.1 %collective-permute-start.14 = (bf16[3,128,256]{2,1,0:T(8,128)(2,1)}, bf16[3,128,256]{2,1,0:T(8,128)(2,1)}, u32[]{:S(2)}, u32[]{:S(2)}) collective-permute-start(bf16[3,128,256]{2,1,0:T(8,128)(2,1)} %get-tuple-element.100), channel_id=1, source_target_pairs={{0,2},{1,3},{2,4},{3,5},{4,6},{5,7},{6,0},{7,1},{8,10},{9,11},{10,... | collective-permute-start | bytes 589832 | tf_op jit(solution)/shard_map/ppermute | solution.py:46
  103.7 15.8 %collective-permute-start.16 = (bf16[3,128,256]{2,1,0:T(8,128)(2,1)}, bf16[3,128,256]{2,1,0:T(8,128)(2,1)}, u32[]{:S(2)}, u32[]{:S(2)}) collective-permute-start(bf16[3,128,256]{2,1,0:T(8,128)(2,1)} %get-tuple-element.102), channel_id=1, source_target_pairs={{0,6},{1,7},{2,0},{3,1},{4,2},{5,3},{6,4},{7,5},{8,14},{9,15},{10,... | collective-permute-start | bytes 589832 | tf_op jit(solution)/shard_map/ppermute | solution.py:46
  105.0 14.5 %collective-permute-start.18 = (bf16[3,128,256]{2,1,0:T(8,128)(2,1)}, bf16[3,128,256]{2,1,0:T(8,128)(2,1)}, u32[]{:S(2)}, u32[]{:S(2)}) collective-permute-start(bf16[3,128,256]{2,1,0:T(8,128)(2,1)} %get-tuple-element.104), channel_id=1, source_target_pairs={{0,3},{1,2},{2,5},{3,4},{4,7},{5,6},{6,1},{7,0},{8,11},{9,10},{10,... | collective-permute-start | bytes 589832 | tf_op jit(solution)/shard_map/ppermute | solution.py:55
  106.0 13.5 %collective-permute-start.20 = (bf16[3,128,256]{2,1,0:T(8,128)(2,1)}, bf16[3,128,256]{2,1,0:T(8,128)(2,1)}, u32[]{:S(2)}, u32[]{:S(2)}) collective-permute-start(bf16[3,128,256]{2,1,0:T(8,128)(2,1)} %get-tuple-element.106), channel_id=1, source_target_pairs={{0,7},{1,6},{2,1},{3,0},{4,3},{5,2},{6,5},{7,4},{8,15},{9,14},{10,... | collective-permute-start | bytes 589832 | tf_op jit(solution)/shard_map/ppermute | solution.py:55
  112.4 25.5 %all-to-all-start.1 = ((bf16[16,1,16,16,128]{4,3,2,1,0:T(8,128)(2,1)}), bf16[16,1,16,16,128]{4,3,2,1,0:T(8,128)(2,1)S(1)}, u32[]{:S(2)}, u32[]{:S(2)}) async-start(bf16[16,1,16,16,128]{4,3,2,1,0:T(8,128)(2,1)} %get-tuple-element.87), calls=%async_computation.1 | async-start | bytes 2097152 | tf_op jit(solution)/shard_map/all_to_all | solution.py:556
  121.5 4.7 %collective-permute-start.21 = (bf16[4,3,128,256]{3,2,1,0:T(8,128)(2,1)}, bf16[4,3,128,256]{3,2,1,0:T(8,128)(2,1)S(1)}, u32[]{:S(2)}, u32[]{:S(2)}) collective-permute-start(bf16[4,3,128,256]{3,2,1,0:T(8,128)(2,1)} %get-tuple-element.109), channel_id=1, source_target_pairs={{0,1},{1,0},{2,3},{3,2},{4,5},{5,4},{6,7},{7,6},{8,9},{9,8},{10,11... | collective-permute-start | bytes 2359304 | tf_op jit(solution)/shard_map/ppermute | solution.py:50
  122.8 8.3 %collective-permute-start.15 = (bf16[3,128,256]{2,1,0:T(8,128)(2,1)}, bf16[3,128,256]{2,1,0:T(8,128)(2,1)}, u32[]{:S(2)}, u32[]{:S(2)}) collective-permute-start(bf16[3,128,256]{2,1,0:T(8,128)(2,1)} %get-tuple-element.101), channel_id=1, source_target_pairs={{0,4},{1,5},{2,6},{3,7},{4,0},{5,1},{6,2},{7,3},{8,12},{9,13},{10,... | collective-permute-start | bytes 589832 | tf_op jit(solution)/shard_map/ppermute | solution.py:46
  123.2 7.9 %collective-permute-start.17 = (bf16[3,128,256]{2,1,0:T(8,128)(2,1)}, bf16[3,128,256]{2,1,0:T(8,128)(2,1)}, u32[]{:S(2)}, u32[]{:S(2)}) collective-permute-start(bf16[3,128,256]{2,1,0:T(8,128)(2,1)} %get-tuple-element.103), channel_id=1, source_target_pairs={{0,1},{1,0},{2,3},{3,2},{4,5},{5,4},{6,7},{7,6},{8,9},{9,8},{10,11... | collective-permute-start | bytes 589832 | tf_op jit(solution)/shard_map/ppermute | solution.py:55
  123.6 11.9 %collective-permute-start.19 = (bf16[3,128,256]{2,1,0:T(8,128)(2,1)}, bf16[3,128,256]{2,1,0:T(8,128)(2,1)}, u32[]{:S(2)}, u32[]{:S(2)}) collective-permute-start(bf16[3,128,256]{2,1,0:T(8,128)(2,1)} %get-tuple-element.105), channel_id=1, source_target_pairs={{0,5},{1,4},{2,7},{3,6},{4,1},{5,0},{6,3},{7,2},{8,13},{9,12},{10,... | collective-permute-start | bytes 589832 | tf_op jit(solution)/shard_map/ppermute | solution.py:55
  (13 other events, 91.4 us)
where the time goes:
time: 142 us; the launch traced here: 141 us
  Pallas kernels  66 us (46%)
  starting transfers between devices  46.6 us (33%)
  waiting for transfers between devices  21.3 us (15%)
  local copies, waits for them, and re-layouts  4.64 us (3%)
  other arithmetic  1.63 us (1%)
    pallas_call x2, Pallas kernels, backward(): pl.pallas_call(functools.partial(backward_kernel, by_chip), out_shape=[ja...  26 us
    pallas_call x2, Pallas kernels, forward(): pl.pallas_call(forward_kernel, out_shape=[jax.ShapeDtypeStruct(out, jnp.b...  21.5 us
    ppermute x8, waiting for transfers between devices, turn_across(): return lax.ppermute(x, 'seq', pairs)  18.2 us
    ppermute x8, starting transfers between devices, turn_across(): return lax.ppermute(x, 'seq', pairs)  13.1 us
    ppermute x12, starting transfers between devices, turn(): return lax.ppermute(x, 'seq', pairs)  13 us
    all_to_all x1, starting transfers between devices, local(): lax.all_to_all(out.reshape(groups * PEERS * CHUNKS, 16, HEAD_DIM), ('dp',...  10.6 us
    pallas_call x3, Pallas kernels, copy_kernel(): pl.pallas_call(kernel, out_shape=[jax.ShapeDtypeStruct(x, jnp.bfloat16) f...  8.62 us
    all_to_all x1, starting transfers between devices, local(): lax.all_to_all(slots, 'dp', split_axis=0, concat_axis=0, tiled=True)  7.11 us
  transfers between devices with their start and end apart: 24, of which 6 were waited for; matrix products, arithmetic and copies ran while one was open for 1% of the time, Pallas kernels for 42%

commit v1 on v0

--- a/solution.py
+++ b/solution.py
@@ -57,7 +57,6 @@
 
 def turn_direct(parts):
     own, sib = list(parts[:CHIPS]), list(parts[CHIPS:])
-    sib[0] = turn_across(sib[0], 0)
     for d in (1, 3, 2):
         own[d], sib[d] = turn(own[d], d), turn_across(sib[d], d)
     return own, sib
@@ -131,26 +130,29 @@
 
 def pack(arrays, k, slabs, after):
     n, rows = len(arrays), arrays[0].shape[0]
+    parts = [(d, sib) for d in (1, 3, 2, 0) for sib in range(CORES) if (d, sib) != (0, 1)]
 
     def plan(ins, outs):
         y, c = position()
         return [
             (
                 ins[a].at[:, pl.ds(column(chip(y, d), 1 - c if sib else c, k), WIDTH)],
-                outs[sib * CHIPS + d].at[a],
+                outs[i].at[a],
             )
-            for d in (1, 3, 0, 2)
-            for sib in range(CORES)
+            for i, (d, sib) in enumerate(parts)
             for a in range(n)
         ] + [
-            (ins[a].at[:, pl.ds(column(chip(y, d), 1 - c, k), WIDTH)], outs[PEERS].at[d, i])
-            for d in range(CHIPS)
-            for i, (a, k) in enumerate(slabs)
+            (ins[a].at[:, pl.ds(column(chip(y, d), 1 - c, j), WIDTH)], outs[-1].at[o, i])
+            for o, d in enumerate(list(range(CHIPS)) + [0])
+            for i, (a, j) in enumerate(slabs if o < CHIPS else [(a, k) for a, _ in slabs])
         ]
 
-    shapes = [(n, rows, WIDTH)] * PEERS + [(CHIPS, len(slabs), rows, WIDTH)]
-    pieces = [(rows, WIDTH)] * (PEERS * n + CHIPS * len(slabs))
-    return copy_kernel(plan, arrays, shapes, pieces, after)
+    shapes = [(n, rows, WIDTH)] * len(parts) + [(CHIPS + 1, len(slabs), rows, WIDTH)]
+    pieces = [(rows, WIDTH)] * (len(parts) * n + (CHIPS + 1) * len(slabs))
+    (*outs, other), token = copy_kernel(plan, arrays, shapes, pieces, after)
+    by_part = dict(zip(parts, outs))
+    own = [by_part[d, 0] for d in range(CHIPS)]
+    return own + [None] + [by_part[d, 1] for d in (1, 2, 3)], other, token
 
 
 def merge_columns(arrays, swapped, slabs, after):
@@ -171,12 +173,13 @@
     return copy_kernel(plan, list(arrays) + [swapped], shapes, pieces, after)
 
 
-def pick_other_core_rows(got, after):
+def pick_other_core_rows(got, last, after):
     def plan(ins, outs):
-        return [(ins[d].at[1], outs[0].at[d]) for d in range(CHIPS)]
+        return [(ins[d].at[1], outs[0].at[d]) for d in range(CHIPS)] + [(ins[-1], outs[0].at[CHIPS])]
 
     shape = got[0].shape[1:]
-    return copy_kernel(plan, got, [(CHIPS,) + shape], [shape] * CHIPS, after)
+    inputs = list(got) + [last]
+    return copy_kernel(plan, inputs, [(CHIPS + 1,) + shape], [shape] * (CHIPS + 1), after)
 
 
 def unpack(own, sib, into, k, after):
@@ -530,14 +533,19 @@
     inputs = [queries, keys, values, grad_mixed]
 
     slabs = [(a, 1) for a in range(4)]
-    (*parts, other), token = pack(inputs, 0, slabs, [])
+    parts, other, token = pack(inputs, 0, slabs, [])
     own, sib = turn_direct(parts)
-    second, token = merge_columns(inputs, swap_cores(other), slabs, token)
+    swapped = swap_cores(other)
+    second, token = merge_columns(inputs, swapped, slabs, token)
     second = turn_all(second)
 
-    pieces = [at_first(x, 0, 3) for x in own + sib]
+    def chunk0(count):
+        by_d = [at_first(x, 0, count) for x in own + sib[1:]]
+        return by_d[:CHIPS] + [at_slabs(swapped, CHIPS, 0, count)] + by_d[CHIPS:]
+
+    pieces = chunk0(3)
     out, saved, token = forward(pieces, scalars, None, 0, token)
-    pieces = [at_first(x, 0, 4) for x in own + sib]
+    pieces = chunk0(4)
     got, token = backward(pieces, saved, scalars, True, token)
     got = turn_all(got)
 
@@ -552,17 +560,19 @@
     parts = gate(parts, token + got[1:])
     own, sib = turn_direct(parts)
 
+    (other,), token = pick_other_core_rows(got, sib[0], token)
+    other = swap_cores(other)
     slots, token = pick([spread.reshape(groups, PEERS * CHUNKS, 16, HEAD_DIM)], sender, token)
     landed = lax.all_to_all(slots, "dp", split_axis=0, concat_axis=0, tiled=True)
     landed = landed.reshape(groups, PEERS, CHUNKS, 16, HEAD_DIM)
 
     near = [own[1], sib[1], own[3], sib[3]]
-    (other,), token = pick_other_core_rows(got, token + near)
-    other = swap_cores(other)
     grads, token = unpack(
-        [(x, 0) for x in got], [(other, d) for d in range(CHIPS)], None, 0, token
+        [(x, 0) for x in got], [(other, d) for d in range(CHIPS)], None, 0, token + near
     )
-    grads, token = unpack([(x, None) for x in own], [(x, None) for x in sib], grads, 1, token)
+    grads, token = unpack(
+        [(x, None) for x in own], [(other, CHIPS)] + [(x, None) for x in sib[1:]], grads, 1, token
+    )
     mixed, token = settle(landed, token)
     return (mixed, grads[0], grads[1], grads[2])
 

time: 142 us -> 141 us (level)
  waiting for transfers between devices: 21.3 us -> 16 us
  starting transfers between devices: 46.6 us -> 49.9 us
    ppermute x8 -> x6, waiting for transfers between devices: 18.2 us -> 9.78 us  [turn_across(): return lax.ppermute(x, 'seq', pairs)]
    ppermute x12, starting transfers between devices: 13 us -> 17.5 us  [turn(): return lax.ppermute(x, 'seq', pairs)]
    ppermute x8 -> x6, starting transfers between devices: 13.1 us -> 15.9 us  [turn_across(): return lax.ppermute(x, 'seq', pairs)]
    all_to_all x1, starting transfers between devices: 7.11 us -> 5.09 us  [local(): lax.all_to_all(slots, 'dp', split_axis=0, concat_axis=0, tiled=True)]
    all_to_all x1, starting transfers between devices: 10.6 us -> 8.79 us  [local(): lax.all_to_all(out.reshape(groups * PEERS * CHUNKS, 16, HEAD_DIM), ('dp',...]
    ppermute x12, waiting for transfers between devices: 3.05 us -> 4.89 us  [turn(): return lax.ppermute(x, 'seq', pairs)]
    unnamed x27 -> x31, local copies, waits for them, and re-layouts: 4.57 us -> 4.56 us
  transfers between devices with their start and end apart: 24 -> 22, of which waited for: 6 -> 8; matrix products, arithmetic and copies ran while one was open for 1% -> 1% of each run, Pallas kernels for 42% -> 43%
where the time goes in v1:
time: 141 us; the launch traced here: 139 us
  Pallas kernels  65.9 us (47%)
  starting transfers between devices  49.9 us (35%)
  waiting for transfers between devices  16 us (11%)
  local copies, waits for them, and re-layouts  4.63 us (3%)
  other arithmetic  1.76 us (1%)
    pallas_call x2, Pallas kernels, backward(): pl.pallas_call(functools.partial(backward_kernel, by_chip), out_shape=[ja...  25.9 us
    pallas_call x2, Pallas kernels, forward(): pl.pallas_call(forward_kernel, out_shape=[jax.ShapeDtypeStruct(out, jnp.b...  21.5 us
    ppermute x12, starting transfers between devices, turn(): return lax.ppermute(x, 'seq', pairs)  17.5 us
    ppermute x6, starting transfers between devices, turn_across(): return lax.ppermute(x, 'seq', pairs)  15.9 us
    ppermute x6, waiting for transfers between devices, turn_across(): return lax.ppermute(x, 'seq', pairs)  9.78 us
    all_to_all x1, starting transfers between devices, local(): lax.all_to_all(out.reshape(groups * PEERS * CHUNKS, 16, HEAD_DIM), ('dp',...  8.79 us
    pallas_call x3, Pallas kernels, copy_kernel(): pl.pallas_call(kernel, out_shape=[jax.ShapeDtypeStruct(x, jnp.bfloat16) f...  8.68 us
    all_to_all x1, starting transfers between devices, local(): lax.all_to_all(slots, 'dp', split_axis=0, concat_axis=0, tiled=True)  5.09 us
  transfers between devices with their start and end apart: 22, of which 8 were waited for; matrix products, arithmetic and copies ran while one was open for 1% of the time, Pallas kernels for 43%

profile of v1, /device:TPU:1, one launch (start us, length us, event | category | flops | bytes accessed | tf_op | source)
XLA Modules:
  0.0 139.1 jit_solution(695501589559925467)
XLA Ops:
  0.7 4.0 %shard_map.93 = (bf16[4,128,256]{2,1,0:T(8,128)(2,1)}, bf16[4,128,256]{2,1,0:T(8,128)(2,1)}, bf16[4,128,256]{2,1,0:T(8,128)(2,1)}, bf16[4,128,256]{2,1,0:T(8,128...) custom-call(bf16[128,4096]{1,0:T(8,128)(2,1)} %refs_0_.3, ...), custom_call_target="tpu_custom_call" | custom-call | flops 55000000 | bytes 65536 | tf_op jit(solution)/shard_map/pallas_call | solution.py:103
  7.5 2.6 %collective-permute-start.5 = (bf16[4,128,256]{2,1,0:T(8,128)(2,1)}, bf16[4,128,256]{2,1,0:T(8,128)(2,1)S(1)}, u32[]{:S(2)}, u32[]{:S(2)}) collective-permute-start(bf16[4,128,256]{2,1,0:T(8,128)(2,1)} %get-tuple-element.69), channel_id=1, source_target_pairs={{0,4},{1,5},{2,6},{3,7},{4,0},{5,1},{6,2},{7,3},{8,12},{9,13},{10,... | collective-permute-start | bytes 786440 | tf_op jit(solution)/shard_map/ppermute | solution.py:46
  13.0 2.8 %collective-permute-done.4.refs_1_ = bf16[4,128,256]{2,1,0:T(8,128)(2,1)S(1)} collective-permute-done((bf16[4,128,256]{2,1,0:T(8,128)(2,1)}, bf16[4,128,256]{2,1,0:T(8,128)(2,1)S(1)}, u32[]{:S(2)}, u32[]{:S(2)}) %collective-permute-start.4) | collective-permute-done | bytes 262176 | tf_op jit(solution)/shard_map/ppermute | solution.py:46
  15.7 8.3 %collective-permute-start.8 = (bf16[4,128,256]{2,1,0:T(8,128)(2,1)}, bf16[4,128,256]{2,1,0:T(8,128)(2,1)}, u32[]{:S(2)}, u32[]{:S(2)}) collective-permute-start(bf16[4,128,256]{2,1,0:T(8,128)(2,1)} %get-tuple-element.72), channel_id=1, source_target_pairs={{0,5},{1,4},{2,7},{3,6},{4,1},{5,0},{6,3},{7,2},{8,13},{9,12},{10,... | collective-permute-start | bytes 786440 | tf_op jit(solution)/shard_map/ppermute | solution.py:55
  25.1 2.7 %shard_map.94 = (bf16[2,4,128,256]{3,2,1,0:T(8,128)(2,1)}, bf16[2,4,128,256]{3,2,1,0:T(8,128)(2,1)}, bf16[2,4,128,256]{3,2,1,0:T(8,128)(2,1)}, bf16[2,4,128,256]{3,2,1,0:T(8,128)(2,1)}, f32[8,128]{1,0:T(8,128)}) custom-call(bf16[128,4096]{1,0:T(8,128)(2,1)} %refs_0_.3, bf16[128,4096]{1,0:T(8,128)(2,1)} %refs_1_.3, bf16[128,4096]{1,0:T(8,128)(2,1)} %refs_2_.3, ...), custom_call_target="tpu_custom_call" | custom-call | flops 55000000 | bytes 65536 | tf_op jit(solution)/shard_map/pallas_call | solution.py:103
  30.6 3.8 %collective-permute-done.8.refs_6_ = bf16[4,128,256]{2,1,0:T(8,128)(2,1)} collective-permute-done((bf16[4,128,256]{2,1,0:T(8,128)(2,1)}, bf16[4,128,256]{2,1,0:T(8,128)(2,1)}, u32[]{:S(2)}, u32[]{:S(2)}) %collective-permute-start.8) | collective-permute-done | bytes 262176 | tf_op jit(solution)/shard_map/ppermute | solution.py:55
  34.4 10.8 %shard_map.95 = (bf16[16,8,2,16,128]{4,3,2,1,0:T(8,128)(2,1)}, bf16[2,4,3,256,256]{4,3,2,1,0:T(8,128)(2,1)}, bf16[2,4,3,256,256]{4,3,2,1,0:T(8,128)(2,1)}, f32[8,128]{1,0:T(8,128)}) custom-call(s32[14]{0:T(128)} %pad_add_fusion.scalars_ref, bf16[4,128,256]{2,1,0:T(8,128)(2,1)} %get-tuple-element.67.refs_0_, bf16[4,128,256]{2,1,0:T(8,128)(2,1)} %copy-done.10, ...), custom_call_target="tpu_custom_call" | custom-call | flops 55000000 | bytes 65536 | tf_op jit(solution)/shard_map/pallas_call | solution.py:453
  45.2 12.9 %shard_map.96 = (bf16[2,3,128,256]{3,2,1,0:T(8,128)(2,1)}, bf16[2,3,128,256]{3,2,1,0:T(8,128)(2,1)}, bf16[2,3,128,256]{3,2,1,0:T(8,128)(2,1)}, bf16[2,3,128,256]{3,2,1,0:T(8,128)(2,1)}, f32[8,128]{1,0:T(8,128)}) custom-call(s32[14]{0:T(128)} %pad_add_fusion.scalars_ref, bf16[4,128,256]{2,1,0:T(8,128)(2,1)} %get-tuple-element.67.refs_0_, ...), custom_call_target="tpu_custom_call" | custom-call | flops 16499999744 | bytes 65536 | tf_op jit(solution)/shard_map/pallas_call | solution.py:477
  58.1 2.6 %collective-permute-start.10 = (bf16[2,3,128,256]{3,2,1,0:T(8,128)(2,1)}, bf16[2,3,128,256]{3,2,1,0:T(8,128)(2,1)S(1)}, u32[]{:S(2)}, u32[]{:S(2)}) collective-permute-start(bf16[2,3,128,256]{3,2,1,0:T(8,128)(2,1)} %get-tuple-element.82), channel_id=1, source_target_pairs={{0,2},{1,3},{2,4},{3,5},{4,6},{5,7},{6,0},{7,1},{8,10},{9,11},{10,... | collective-permute-start | bytes 1179656 | tf_op jit(solution)/shard_map/ppermute | solution.py:46
  61.6 1.6 %collective-permute-start.12 = (bf16[2,3,128,256]{3,2,1,0:T(8,128)(2,1)}, bf16[2,3,128,256]{3,2,1,0:T(8,128)(2,1)}, u32[]{:S(2)}, u32[]{:S(2)}) collective-permute-start(bf16[2,3,128,256]{3,2,1,0:T(8,128)(2,1)} %get-tuple-element.84), channel_id=1, source_target_pairs={{0,6},{1,7},{2,0},{3,1},{4,2},{5,3},{6,4},{7,5},{8,14},{9,15},{10,... | collective-permute-start | bytes 1179656 | tf_op jit(solution)/shard_map/ppermute | solution.py:46
  64.0 10.8 %shard_map.97 = (bf16[16,8,2,16,128]{4,3,2,1,0:T(8,128)(2,1)}, bf16[2,4,3,256,256]{4,3,2,1,0:T(8,128)(2,1)}, bf16[2,4,3,256,256]{4,3,2,1,0:T(8,128)(2,1)}, f32[8,128]{1,0:T(8,128)}) custom-call(s32[14]{0:T(128)} %pad_add_fusion.scalars_ref, bf16[2,4,128,256]{3,2,1,0:T(8,128)(2,1)} %get-tuple-element.63.refs_0_.refs_4_, ...), custom_call_target="tpu_custom_call", output_to_operand_aliasing={{0}: (9, {})} | custom-call | flops 11000000512 | bytes 65536 | tf_op jit(solution)/shard_map/pallas_call | solution.py:453
  74.7 8.8 %all-to-all-start = ((bf16[256,16,128]{2,1,0:T(8,128)(2,1)}), bf16[256,16,128]{2,1,0:T(8,128)(2,1)S(1)}, u32[]{:S(2)}, u32[]{:S(2)}) async-start(bf16[256,16,128]{2,1,0:T(8,128)(2,1)} %bitcast.18), calls=%async_computation | async-start | bytes 2097152 | tf_op jit(solution)/shard_map/all_to_all | solution.py:554
  83.5 13.0 %shard_map.98 = (bf16[3,128,256]{2,1,0:T(8,128)(2,1)}, bf16[3,128,256]{2,1,0:T(8,128)(2,1)}, bf16[3,128,256]{2,1,0:T(8,128)(2,1)}, bf16[3,128,256]{2,1,0:T(8,128...) custom-call(s32[14]{0:T(128)} %pad_add_fusion.scalars_ref, ...), custom_call_target="tpu_custom_call" | custom-call | flops 16499999744 | bytes 65536 | tf_op jit(solution)/shard_map/pallas_call | solution.py:477
  97.4 2.0 %shard_map.100 = (bf16[5,3,128,256]{3,2,1,0:T(8,128)(2,1)}, f32[8,128]{1,0:T(8,128)}) custom-call(bf16[2,3,128,256]{3,2,1,0:T(8,128)(2,1)} %get-tuple-element.81.refs_0_, bf16[2,3,128,256]{3,2,1,0:T(8,128)(2,1)} %copy-done.4, bf16[2,3,128,256]{3,2,1,0:T(8,128)(2,1)} %copy-done.5, bf16[2,3,128,256]{3,2,1,0:T(8,128)(2,1)} %collective-permute-done.12.refs_11_.refs_3_, ...), custom_call_target="tpu_custom_call" | custom-call | flops 55000000 | bytes 65536 | tf_op jit(solution)/shard_map/pallas_call | solution.py:103
  103.4 2.9 %shard_map.101 = (bf16[16,1,16,16,128]{4,3,2,1,0:T(8,128)(2,1)}, f32[8,128]{1,0:T(8,128)}) custom-call(s32[16]{0:T(128)} %broadcast_clamp_fusion.sender_ref, bf16[16,16,16,128]{3,2,1,0:T(8,128)(2,1)} %bitcast.17, f32[8,128]{1,0:T(8,128)} %get-tuple-element.98.refs_1_), custom_call_target="tpu_custom_call" | custom-call | flops 55000000 | bytes 65536 | tf_op jit(solution)/shard_map/pallas_call | solution.py:251
  106.3 5.1 %all-to-all-start.1 = ((bf16[16,1,16,16,128]{4,3,2,1,0:T(8,128)(2,1)}), bf16[16,1,16,16,128]{4,3,2,1,0:T(8,128)(2,1)S(1)}, u32[]{:S(2)}, u32[]{:S(2)}) async-start(bf16[16,1,16,16,128]{4,3,2,1,0:T(8,128)(2,1)} %get-tuple-element.99), calls=%async_computation.1 | async-start | bytes 2097152 | tf_op jit(solution)/shard_map/all_to_all | solution.py:566
  115.2 2.0 %collective-permute-start.19 = (bf16[3,128,256]{2,1,0:T(8,128)(2,1)}, bf16[3,128,256]{2,1,0:T(8,128)(2,1)S(1)}, u32[]{:S(2)}, u32[]{:S(2)}) collective-permute-start(bf16[3,128,256]{2,1,0:T(8,128)(2,1)} %get-tuple-element.107), channel_id=1, source_target_pairs={{0,7},{1,6},{2,1},{3,0},{4,3},{5,2},{6,5},{7,4},{8,15},{9,14},{10,... | collective-permute-start | bytes 589832 | tf_op jit(solution)/shard_map/ppermute | solution.py:55
  117.3 1.8 %collective-permute-done.13.refs_6_.refs_1_ = bf16[3,128,256]{2,1,0:T(8,128)(2,1)S(1)} collective-permute-done((bf16[3,128,256]{2,1,0:T(8,128)(2,1)}, bf16[3,128,256]{2,1,0:T(8,128)(2,1)S(1)}, u32[]{:S(2)}, u32[]{:S(2)}) %collective-permute-start.13) | collective-permute-done | bytes 196640 | tf_op jit(solution)/shard_map/ppermute | solution.py:46
  119.1 1.6 %collective-permute-start.14 = (bf16[3,128,256]{2,1,0:T(8,128)(2,1)}, bf16[3,128,256]{2,1,0:T(8,128)(2,1)}, u32[]{:S(2)}, u32[]{:S(2)}) collective-permute-start(bf16[3,128,256]{2,1,0:T(8,128)(2,1)} %get-tuple-element.102), channel_id=1, source_target_pairs={{0,4},{1,5},{2,6},{3,7},{4,0},{5,1},{6,2},{7,3},{8,12},{9,13},{10,... | collective-permute-start | bytes 589832 | tf_op jit(solution)/shard_map/ppermute | solution.py:46
  120.7 3.4 %collective-permute-start.18 = (bf16[3,128,256]{2,1,0:T(8,128)(2,1)}, bf16[3,128,256]{2,1,0:T(8,128)(2,1)}, u32[]{:S(2)}, u32[]{:S(2)}) collective-permute-start(bf16[3,128,256]{2,1,0:T(8,128)(2,1)} %get-tuple-element.106), channel_id=1, source_target_pairs={{0,5},{1,4},{2,7},{3,6},{4,1},{5,0},{6,3},{7,2},{8,13},{9,12},{10,... | collective-permute-start | bytes 589832 | tf_op jit(solution)/shard_map/ppermute | solution.py:55
  126.0 2.4 %shard_map.102 = (bf16[128,4096]{1,0:T(8,128)(2,1)}, bf16[128,4096]{1,0:T(8,128)(2,1)}, bf16[128,4096]{1,0:T(8,128)(2,1)}, f32[8,128]{1,0:T(8,128)}) custom-call(bf16[2,3,128,256]{3,2,1,0:T(8,128)(2,1)} %get-tuple-element.81.refs_0_, bf16[2,3,128,256]{3,2,1,0:T(8,128)(2,1)} %copy-done.4, bf16[2,3,128,256]{3,2,1,0:T(8,128)(2,1)} %copy-done.5, ...), custom_call_target="tpu_custom_call" | custom-call | flops 55000000 | bytes 65536 | tf_op jit(solution)/shard_map/pallas_call | solution.py:217
  128.7 4.8 %collective-permute-done.18.refs_6_ = bf16[3,128,256]{2,1,0:T(8,128)(2,1)} collective-permute-done((bf16[3,128,256]{2,1,0:T(8,128)(2,1)}, bf16[3,128,256]{2,1,0:T(8,128)(2,1)}, u32[]{:S(2)}, u32[]{:S(2)}) %collective-permute-start.18) | collective-permute-done | bytes 196640 | tf_op jit(solution)/shard_map/ppermute | solution.py:55
  133.5 2.4 %shard_map.103 = (bf16[128,4096]{1,0:T(8,128)(2,1)}, bf16[128,4096]{1,0:T(8,128)(2,1)}, bf16[128,4096]{1,0:T(8,128)(2,1)}, f32[8,128]{1,0:T(8,128)}) custom-call(bf16[3,128,256]{2,1,0:T(8,128)(2,1)} %get-tuple-element.100.refs_0_, bf16[3,128,256]{2,1,0:T(8,128)(2,1)} %copy-done.6, ...), custom_call_target="tpu_custom_call", output_to_operand_aliasing={{0}: (8, {}), {1}: (9, {}), {2}: (10, {})} | custom-call | flops 55000000 | bytes 65536 | tf_op jit(solution)/shard_map/pallas_call | solution.py:217
  137.0 2.1 %shard_map.104 = (bf16[128,4096]{1,0:T(8,128)(2,1)}, f32[8,128]{1,0:T(8,128)}) custom-call(bf16[2,8,8,2,16,128]{5,4,3,2,1,0:T(8,128)(2,1)} %bitcast.16, f32[8,128]{1,0:T(8,128)} %get-tuple-element.113.refs_0_), custom_call_target="tpu_custom_call" | custom-call | flops 55000000 | bytes 65536 | tf_op jit(solution)/shard_map/pallas_call | solution.py:287
  (73 shorter events, 23.1 us)
Async XLA Ops:
  0.6 24.2 %copy-start.14 = (s32[16]{0:T(128)S(1)}, s32[16]{0:T(128)}, u32[]{:S(2)}) copy-start(s32[16]{0:T(128)} %param.11) | copy-start | bytes 196
  4.6 19.4 %collective-permute-start = (bf16[5,4,128,256]{3,2,1,0:T(8,128)(2,1)}, bf16[5,4,128,256]{3,2,1,0:T(8,128)(2,1)S(1)}, u32[]{:S(2)}, u32[]{:S(2)}) collective-permute-start(bf16[5,4,128,256]{3,2,1,0:T(8,128)(2,1)} %get-tuple-element.61), channel_id=1, source_target_pairs={{0,1},{1,0},{2,3},{3,2},{4,5},{5,4},{6,7},{7,6},{8,9},{9,8},{10,11... | collective-permute-start | bytes 3932168 | tf_op jit(solution)/shard_map/ppermute | solution.py:50
  6.1 9.6 %collective-permute-start.4 = (bf16[4,128,256]{2,1,0:T(8,128)(2,1)}, bf16[4,128,256]{2,1,0:T(8,128)(2,1)S(1)}, u32[]{:S(2)}, u32[]{:S(2)}) collective-permute-start(bf16[4,128,256]{2,1,0:T(8,128)(2,1)} %get-tuple-element.68), channel_id=1, source_target_pairs={{0,2},{1,3},{2,4},{3,5},{4,6},{5,7},{6,0},{7,1},{8,10},{9,11},{10,... | collective-permute-start | bytes 786440 | tf_op jit(solution)/shard_map/ppermute | solution.py:46
  7.5 20.3 %collective-permute-start.5 = (bf16[4,128,256]{2,1,0:T(8,128)(2,1)}, bf16[4,128,256]{2,1,0:T(8,128)(2,1)S(1)}, u32[]{:S(2)}, u32[]{:S(2)}) collective-permute-start(bf16[4,128,256]{2,1,0:T(8,128)(2,1)} %get-tuple-element.69), channel_id=1, source_target_pairs={{0,4},{1,5},{2,6},{3,7},{4,0},{5,1},{6,2},{7,3},{8,12},{9,13},{10,... | collective-permute-start | bytes 786440 | tf_op jit(solution)/shard_map/ppermute | solution.py:46
  10.2 17.7 %collective-permute-start.6 = (bf16[4,128,256]{2,1,0:T(8,128)(2,1)}, bf16[4,128,256]{2,1,0:T(8,128)(2,1)}, u32[]{:S(2)}, u32[]{:S(2)}) collective-permute-start(bf16[4,128,256]{2,1,0:T(8,128)(2,1)} %get-tuple-element.70), channel_id=1, source_target_pairs={{0,6},{1,7},{2,0},{3,1},{4,2},{5,3},{6,4},{7,5},{8,14},{9,15},{10,... | collective-permute-start | bytes 786440 | tf_op jit(solution)/shard_map/ppermute | solution.py:46
  11.2 17.9 %collective-permute-start.7 = (bf16[4,128,256]{2,1,0:T(8,128)(2,1)}, bf16[4,128,256]{2,1,0:T(8,128)(2,1)}, u32[]{:S(2)}, u32[]{:S(2)}) collective-permute-start(bf16[4,128,256]{2,1,0:T(8,128)(2,1)} %get-tuple-element.71), channel_id=1, source_target_pairs={{0,3},{1,2},{2,5},{3,4},{4,7},{5,6},{6,1},{7,0},{8,11},{9,10},{10,... | collective-permute-start | bytes 786440 | tf_op jit(solution)/shard_map/ppermute | solution.py:55
  15.7 18.7 %copy-start.10 = (bf16[4,128,256]{2,1,0:T(8,128)(2,1)}, bf16[4,128,256]{2,1,0:T(8,128)(2,1)S(1)}, u32[]{:S(2)}) copy-start(bf16[4,128,256]{2,1,0:T(8,128)(2,1)S(1)} %collective-permute-done.4.refs_1_) | copy-start | bytes 786436
  15.7 18.7 %collective-permute-start.8 = (bf16[4,128,256]{2,1,0:T(8,128)(2,1)}, bf16[4,128,256]{2,1,0:T(8,128)(2,1)}, u32[]{:S(2)}, u32[]{:S(2)}) collective-permute-start(bf16[4,128,256]{2,1,0:T(8,128)(2,1)} %get-tuple-element.72), channel_id=1, source_target_pairs={{0,5},{1,4},{2,7},{3,6},{4,1},{5,0},{6,3},{7,2},{8,13},{9,12},{10,... | collective-permute-start | bytes 786440 | tf_op jit(solution)/shard_map/ppermute | solution.py:55
  24.1 10.4 %collective-permute-start.9 = (bf16[4,128,256]{2,1,0:T(8,128)(2,1)}, bf16[4,128,256]{2,1,0:T(8,128)(2,1)}, u32[]{:S(2)}, u32[]{:S(2)}) collective-permute-start(bf16[4,128,256]{2,1,0:T(8,128)(2,1)} %get-tuple-element.73), channel_id=1, source_target_pairs={{0,7},{1,6},{2,1},{3,0},{4,3},{5,2},{6,5},{7,4},{8,15},{9,14},{10,... | collective-permute-start | bytes 786440 | tf_op jit(solution)/shard_map/ppermute | solution.py:55
  27.8 33.7 %collective-permute-start.1 = (bf16[2,4,128,256]{3,2,1,0:T(8,128)(2,1)}, bf16[2,4,128,256]{3,2,1,0:T(8,128)(2,1)S(1)}, u32[]{:S(2)}, u32[]{:S(2)}) collective-permute-start(bf16[2,4,128,256]{3,2,1,0:T(8,128)(2,1)} %get-tuple-element.64), channel_id=1, source_target_pairs={{0,2},{1,3},{2,4},{3,5},{4,6},{5,7},{6,0},{7,1},{8,10},{9,11},{10,... | collective-permute-start | bytes 1572872 | tf_op jit(solution)/shard_map/ppermute | solution.py:46
  27.9 35.3 %collective-permute-start.2 = (bf16[2,4,128,256]{3,2,1,0:T(8,128)(2,1)}, bf16[2,4,128,256]{3,2,1,0:T(8,128)(2,1)S(1)}, u32[]{:S(2)}, u32[]{:S(2)}) collective-permute-start(bf16[2,4,128,256]{3,2,1,0:T(8,128)(2,1)} %get-tuple-element.65), channel_id=1, source_target_pairs={{0,4},{1,5},{2,6},{3,7},{4,0},{5,1},{6,2},{7,3},{8,12},{9,13},{10,... | collective-permute-start | bytes 1572872 | tf_op jit(solution)/shard_map/ppermute | solution.py:46
  29.1 34.0 %collective-permute-start.3 = (bf16[2,4,128,256]{3,2,1,0:T(8,128)(2,1)}, bf16[2,4,128,256]{3,2,1,0:T(8,128)(2,1)}, u32[]{:S(2)}, u32[]{:S(2)}) collective-permute-start(bf16[2,4,128,256]{3,2,1,0:T(8,128)(2,1)} %get-tuple-element.66), channel_id=1, source_target_pairs={{0,6},{1,7},{2,0},{3,1},{4,2},{5,3},{6,4},{7,5},{8,14},{9,15},{10,... | collective-permute-start | bytes 1572872 | tf_op jit(solution)/shard_map/ppermute | solution.py:46
  58.1 38.4 %collective-permute-start.10 = (bf16[2,3,128,256]{3,2,1,0:T(8,128)(2,1)}, bf16[2,3,128,256]{3,2,1,0:T(8,128)(2,1)S(1)}, u32[]{:S(2)}, u32[]{:S(2)}) collective-permute-start(bf16[2,3,128,256]{3,2,1,0:T(8,128)(2,1)} %get-tuple-element.82), channel_id=1, source_target_pairs={{0,2},{1,3},{2,4},{3,5},{4,6},{5,7},{6,0},{7,1},{8,10},{9,11},{10,... | collective-permute-start | bytes 1179656 | tf_op jit(solution)/shard_map/ppermute | solution.py:46
  60.7 35.8 %collective-permute-start.11 = (bf16[2,3,128,256]{3,2,1,0:T(8,128)(2,1)}, bf16[2,3,128,256]{3,2,1,0:T(8,128)(2,1)S(1)}, u32[]{:S(2)}, u32[]{:S(2)}) collective-permute-start(bf16[2,3,128,256]{3,2,1,0:T(8,128)(2,1)} %get-tuple-element.83), channel_id=1, source_target_pairs={{0,4},{1,5},{2,6},{3,7},{4,0},{5,1},{6,2},{7,3},{8,12},{9,13},{10,... | collective-permute-start | bytes 1179656 | tf_op jit(solution)/shard_map/ppermute | solution.py:46
  61.6 35.0 %collective-permute-start.12 = (bf16[2,3,128,256]{3,2,1,0:T(8,128)(2,1)}, bf16[2,3,128,256]{3,2,1,0:T(8,128)(2,1)}, u32[]{:S(2)}, u32[]{:S(2)}) collective-permute-start(bf16[2,3,128,256]{3,2,1,0:T(8,128)(2,1)} %get-tuple-element.84), channel_id=1, source_target_pairs={{0,6},{1,7},{2,0},{3,1},{4,2},{5,3},{6,4},{7,5},{8,14},{9,15},{10,... | collective-permute-start | bytes 1179656 | tf_op jit(solution)/shard_map/ppermute | solution.py:46
  74.7 27.7 %all-to-all-start = ((bf16[256,16,128]{2,1,0:T(8,128)(2,1)}), bf16[256,16,128]{2,1,0:T(8,128)(2,1)S(1)}, u32[]{:S(2)}, u32[]{:S(2)}) async-start(bf16[256,16,128]{2,1,0:T(8,128)(2,1)} %bitcast.18), calls=%async_computation | async-start | bytes 2097152 | tf_op jit(solution)/shard_map/all_to_all | solution.py:554
  99.4 25.9 %collective-permute-start.16 = (bf16[5,3,128,256]{3,2,1,0:T(8,128)(2,1)}, bf16[5,3,128,256]{3,2,1,0:T(8,128)(2,1)}, u32[]{:S(2)}, u32[]{:S(2)}) collective-permute-start(bf16[5,3,128,256]{3,2,1,0:T(8,128)(2,1)} %get-tuple-element.104), channel_id=1, source_target_pairs={{0,1},{1,0},{2,3},{3,2},{4,5},{5,4},{6,7},{7,6},{8,9},{9,8},{10,11... | collective-permute-start | bytes 2949128 | tf_op jit(solution)/shard_map/ppermute | solution.py:50
  106.3 29.7 %all-to-all-start.1 = ((bf16[16,1,16,16,128]{4,3,2,1,0:T(8,128)(2,1)}), bf16[16,1,16,16,128]{4,3,2,1,0:T(8,128)(2,1)S(1)}, u32[]{:S(2)}, u32[]{:S(2)}) async-start(bf16[16,1,16,16,128]{4,3,2,1,0:T(8,128)(2,1)} %get-tuple-element.99), calls=%async_computation.1 | async-start | bytes 2097152 | tf_op jit(solution)/shard_map/all_to_all | solution.py:566
  111.4 7.7 %collective-permute-start.13 = (bf16[3,128,256]{2,1,0:T(8,128)(2,1)}, bf16[3,128,256]{2,1,0:T(8,128)(2,1)S(1)}, u32[]{:S(2)}, u32[]{:S(2)}) collective-permute-start(bf16[3,128,256]{2,1,0:T(8,128)(2,1)} %get-tuple-element.101), channel_id=1, source_target_pairs={{0,2},{1,3},{2,4},{3,5},{4,6},{5,7},{6,0},{7,1},{8,10},{9,11},{10,... | collective-permute-start | bytes 589832 | tf_op jit(solution)/shard_map/ppermute | solution.py:46
  112.9 7.8 %collective-permute-start.15 = (bf16[3,128,256]{2,1,0:T(8,128)(2,1)}, bf16[3,128,256]{2,1,0:T(8,128)(2,1)S(1)}, u32[]{:S(2)}, u32[]{:S(2)}) collective-permute-start(bf16[3,128,256]{2,1,0:T(8,128)(2,1)} %get-tuple-element.103), channel_id=1, source_target_pairs={{0,6},{1,7},{2,0},{3,1},{4,2},{5,3},{6,4},{7,5},{8,14},{9,15},{10,... | collective-permute-start | bytes 589832 | tf_op jit(solution)/shard_map/ppermute | solution.py:46
  114.3 9.9 %collective-permute-start.17 = (bf16[3,128,256]{2,1,0:T(8,128)(2,1)}, bf16[3,128,256]{2,1,0:T(8,128)(2,1)S(1)}, u32[]{:S(2)}, u32[]{:S(2)}) collective-permute-start(bf16[3,128,256]{2,1,0:T(8,128)(2,1)} %get-tuple-element.105), channel_id=1, source_target_pairs={{0,3},{1,2},{2,5},{3,4},{4,7},{5,6},{6,1},{7,0},{8,11},{9,10},{10,... | collective-permute-start | bytes 589832 | tf_op jit(solution)/shard_map/ppermute | solution.py:55
  115.2 10.1 %collective-permute-start.19 = (bf16[3,128,256]{2,1,0:T(8,128)(2,1)}, bf16[3,128,256]{2,1,0:T(8,128)(2,1)S(1)}, u32[]{:S(2)}, u32[]{:S(2)}) collective-permute-start(bf16[3,128,256]{2,1,0:T(8,128)(2,1)} %get-tuple-element.107), channel_id=1, source_target_pairs={{0,7},{1,6},{2,1},{3,0},{4,3},{5,2},{6,5},{7,4},{8,15},{9,14},{10,... | collective-permute-start | bytes 589832 | tf_op jit(solution)/shard_map/ppermute | solution.py:55
  119.1 9.6 %collective-permute-start.14 = (bf16[3,128,256]{2,1,0:T(8,128)(2,1)}, bf16[3,128,256]{2,1,0:T(8,128)(2,1)}, u32[]{:S(2)}, u32[]{:S(2)}) collective-permute-start(bf16[3,128,256]{2,1,0:T(8,128)(2,1)} %get-tuple-element.102), channel_id=1, source_target_pairs={{0,4},{1,5},{2,6},{3,7},{4,0},{5,1},{6,2},{7,3},{8,12},{9,13},{10,... | collective-permute-start | bytes 589832 | tf_op jit(solution)/shard_map/ppermute | solution.py:46
  120.7 12.8 %collective-permute-start.18 = (bf16[3,128,256]{2,1,0:T(8,128)(2,1)}, bf16[3,128,256]{2,1,0:T(8,128)(2,1)}, u32[]{:S(2)}, u32[]{:S(2)}) collective-permute-start(bf16[3,128,256]{2,1,0:T(8,128)(2,1)} %get-tuple-element.106), channel_id=1, source_target_pairs={{0,5},{1,4},{2,7},{3,6},{4,1},{5,0},{6,3},{7,2},{8,13},{9,12},{10,... | collective-permute-start | bytes 589832 | tf_op jit(solution)/shard_map/ppermute | solution.py:55
  (13 other events, 38.1 us)

commit v2 on v1

--- a/solution.py
+++ b/solution.py
@@ -182,8 +182,8 @@
     return copy_kernel(plan, inputs, [(CHIPS + 1,) + shape], [shape] * (CHIPS + 1), after)
 
 
-def unpack(own, sib, into, k, after):
-    flat = list(own) + list(sib)
+def unpack(own, sib, into, k, turns, after):
+    flat = [x[d] for d in turns for x in (own, sib)]
     arrays = []
     for x, _ in flat:
         if not any(x is z for z in arrays):
@@ -191,7 +191,6 @@
     where = [next(i for i, z in enumerate(arrays) if z is x) for x, _ in flat]
     n, rows, width = arrays[0].shape[-3:]
     olds = [] if into is None else list(into)
-    order = [i * CHIPS + d for d in (0, 1, 3, 2) for i in range(CORES)]
 
     def kernel(*refs):
         ins = refs[: len(arrays)]
@@ -199,9 +198,8 @@
         held, arrive, leave = refs[-3:]
         y, c = position()
         into_vmem, out_of = [], []
-        for i in order:
-            core = 1 - c if i >= CHIPS else c
-            col = column(chip(y, -(i % CHIPS)), core, k)
+        for i in range(len(flat)):
+            col = column(chip(y, -turns[i // CORES]), 1 - c if i % CORES else c, k)
             src = ins[where[i]]
             if flat[i][1] is not None:
                 src = src.at[flat[i][1]]
@@ -221,9 +219,9 @@
         in_specs=[ANY] * (len(arrays) + len(olds) + len(after)),
         out_specs=[ANY] * (n + 1),
         scratch_shapes=[
-            pltpu.VMEM((PEERS, n, rows, width), jnp.bfloat16),
-            pltpu.SemaphoreType.DMA((PEERS,)),
-            pltpu.SemaphoreType.DMA((PEERS * n,)),
+            pltpu.VMEM((len(flat), n, rows, width), jnp.bfloat16),
+            pltpu.SemaphoreType.DMA((len(flat),)),
+            pltpu.SemaphoreType.DMA((len(flat) * n,)),
         ],
         compiler_params=pltpu.CompilerParams(vmem_limit_bytes=VMEM),
         input_output_aliases={len(arrays) + a: a for a in range(len(olds))},
@@ -568,12 +566,14 @@
 
     near = [own[1], sib[1], own[3], sib[3]]
     grads, token = unpack(
-        [(x, 0) for x in got], [(other, d) for d in range(CHIPS)], None, 0, token + near
+        [(x, 0) for x in got], [(other, d) for d in range(CHIPS)], None, 0, (0, 1, 3, 2),
+        token + near,
     )
-    grads, token = unpack(
-        [(x, None) for x in own], [(other, CHIPS)] + [(x, None) for x in sib[1:]], grads, 1, token
-    )
+    own = [(x, None) for x in own]
+    sib = [(other, CHIPS)] + [(x, None) for x in sib[1:]]
+    grads, token = unpack(own, sib, grads, 1, (0, 1, 3), token)
     mixed, token = settle(landed, token)
+    grads, token = unpack(own, sib, grads, 1, (2,), token)
     return (mixed, grads[0], grads[1], grads[2])
 
 

time: 141 us -> 145 us (1.028)
  the two profiles are of different devices: /device:TPU:1 before, /device:TPU:27 now
where the time goes in v2:
time: 145 us; the launch traced here: 144 us
  Pallas kernels  61 us (42%)
  starting transfers between devices  49.4 us (34%)
  waiting for transfers between devices  26.6 us (18%)
  local copies, waits for them, and re-layouts  4.42 us (3%)
  other arithmetic  1.62 us (1%)
    pallas_call x2, Pallas kernels, backward(): pl.pallas_call(functools.partial(backward_kernel, by_chip), out_shape=[ja...  22.2 us
    ppermute x6, waiting for transfers between devices, turn_across(): return lax.ppermute(x, 'seq', pairs)  21.6 us
    pallas_call x2, Pallas kernels, forward(): pl.pallas_call(forward_kernel, out_shape=[jax.ShapeDtypeStruct(out, jnp.b...  18.7 us
    all_to_all x1, starting transfers between devices, local(): lax.all_to_all(out.reshape(groups * PEERS * CHUNKS, 16, HEAD_DIM), ('dp',...  15.3 us
    ppermute x6, starting transfers between devices, turn_across(): return lax.ppermute(x, 'seq', pairs)  14.1 us
    ppermute x12, starting transfers between devices, turn(): return lax.ppermute(x, 'seq', pairs)  10.5 us
    pallas_call x3, Pallas kernels, copy_kernel(): pl.pallas_call(kernel, out_shape=[jax.ShapeDtypeStruct(x, jnp.bfloat16) f...  8.69 us
    all_to_all x1, starting transfers between devices, local(): lax.all_to_all(slots, 'dp', split_axis=0, concat_axis=0, tiled=True)  8.23 us
  transfers between devices with their start and end apart: 22, of which 6 were waited for; matrix products, arithmetic and copies ran while one was open for 1% of the time, Pallas kernels for 38%

profile of v2, /device:TPU:27, one launch (start us, length us, event | category | flops | bytes accessed | tf_op | source)
XLA Modules:
  0.0 144.0 jit_solution(16366127164061767691)
XLA Ops:
  0.7 4.0 %shard_map.93 = (bf16[4,128,256]{2,1,0:T(8,128)(2,1)}, bf16[4,128,256]{2,1,0:T(8,128)(2,1)}, bf16[4,128,256]{2,1,0:T(8,128)(2,1)}, bf16[4,128,256]{2,1,0:T(8,128...) custom-call(bf16[128,4096]{1,0:T(8,128)(2,1)} %refs_0_.3, ...), custom_call_target="tpu_custom_call" | custom-call | flops 55000000 | bytes 65536 | tf_op jit(solution)/shard_map/pallas_call | solution.py:103
  5.4 2.3 %collective-permute-start.5 = (bf16[4,128,256]{2,1,0:T(8,128)(2,1)}, bf16[4,128,256]{2,1,0:T(8,128)(2,1)S(1)}, u32[]{:S(2)}, u32[]{:S(2)}) collective-permute-start(bf16[4,128,256]{2,1,0:T(8,128)(2,1)} %get-tuple-element.73), channel_id=1, source_target_pairs={{0,4},{1,5},{2,6},{3,7},{4,0},{5,1},{6,2},{7,3},{8,12},{9,13},{10,... | collective-permute-start | bytes 786440 | tf_op jit(solution)/shard_map/ppermute | solution.py:46
  7.6 3.5 %collective-permute-start.7 = (bf16[4,128,256]{2,1,0:T(8,128)(2,1)}, bf16[4,128,256]{2,1,0:T(8,128)(2,1)}, u32[]{:S(2)}, u32[]{:S(2)}) collective-permute-start(bf16[4,128,256]{2,1,0:T(8,128)(2,1)} %get-tuple-element.75), channel_id=1, source_target_pairs={{0,3},{1,2},{2,5},{3,4},{4,7},{5,6},{6,1},{7,0},{8,11},{9,10},{10,... | collective-permute-start | bytes 786440 | tf_op jit(solution)/shard_map/ppermute | solution.py:55
  11.7 1.8 %collective-permute-done.4.refs_1_ = bf16[4,128,256]{2,1,0:T(8,128)(2,1)S(1)} collective-permute-done((bf16[4,128,256]{2,1,0:T(8,128)(2,1)}, bf16[4,128,256]{2,1,0:T(8,128)(2,1)S(1)}, u32[]{:S(2)}, u32[]{:S(2)}) %collective-permute-start.4) | collective-permute-done | bytes 262176 | tf_op jit(solution)/shard_map/ppermute | solution.py:46
  13.5 6.5 %collective-permute-start.8 = (bf16[4,128,256]{2,1,0:T(8,128)(2,1)}, bf16[4,128,256]{2,1,0:T(8,128)(2,1)}, u32[]{:S(2)}, u32[]{:S(2)}) collective-permute-start(bf16[4,128,256]{2,1,0:T(8,128)(2,1)} %get-tuple-element.76), channel_id=1, source_target_pairs={{0,5},{1,4},{2,7},{3,6},{4,1},{5,0},{6,3},{7,2},{8,13},{9,12},{10,... | collective-permute-start | bytes 786440 | tf_op jit(solution)/shard_map/ppermute | solution.py:55
  21.6 2.7 %shard_map.94 = (bf16[2,4,128,256]{3,2,1,0:T(8,128)(2,1)}, bf16[2,4,128,256]{3,2,1,0:T(8,128)(2,1)}, bf16[2,4,128,256]{3,2,1,0:T(8,128)(2,1)}, bf16[2,4,128,256]{3,2,1,0:T(8,128)(2,1)}, f32[8,128]{1,0:T(8,128)}) custom-call(bf16[128,4096]{1,0:T(8,128)(2,1)} %refs_0_.3, bf16[128,4096]{1,0:T(8,128)(2,1)} %refs_1_.3, bf16[128,4096]{1,0:T(8,128)(2,1)} %refs_2_.3, ...), custom_call_target="tpu_custom_call" | custom-call | flops 55000000 | bytes 65536 | tf_op jit(solution)/shard_map/pallas_call | solution.py:103
  24.3 2.7 %collective-permute-start.1 = (bf16[2,4,128,256]{3,2,1,0:T(8,128)(2,1)}, bf16[2,4,128,256]{3,2,1,0:T(8,128)(2,1)S(1)}, u32[]{:S(2)}, u32[]{:S(2)}) collective-permute-start(bf16[2,4,128,256]{3,2,1,0:T(8,128)(2,1)} %get-tuple-element.68), channel_id=1, source_target_pairs={{0,2},{1,3},{2,4},{3,5},{4,6},{5,7},{6,0},{7,1},{8,10},{9,11},{10,... | collective-permute-start | bytes 1572872 | tf_op jit(solution)/shard_map/ppermute | solution.py:46
  27.7 5.5 %collective-permute-done.9.refs_7_ = bf16[4,128,256]{2,1,0:T(8,128)(2,1)} collective-permute-done((bf16[4,128,256]{2,1,0:T(8,128)(2,1)}, bf16[4,128,256]{2,1,0:T(8,128)(2,1)}, u32[]{:S(2)}, u32[]{:S(2)}) %collective-permute-start.9) | collective-permute-done | bytes 262176 | tf_op jit(solution)/shard_map/ppermute | solution.py:55
  33.1 9.3 %shard_map.95 = (bf16[16,8,2,16,128]{4,3,2,1,0:T(8,128)(2,1)}, bf16[2,4,3,256,256]{4,3,2,1,0:T(8,128)(2,1)}, bf16[2,4,3,256,256]{4,3,2,1,0:T(8,128)(2,1)}, f32[8,128]{1,0:T(8,128)}) custom-call(s32[14]{0:T(128)} %pad_add_fusion.scalars_ref, bf16[4,128,256]{2,1,0:T(8,128)(2,1)} %get-tuple-element.71.refs_0_, bf16[4,128,256]{2,1,0:T(8,128)(2,1)} %copy-done.10, ...), custom_call_target="tpu_custom_call" | custom-call | flops 55000000 | bytes 65536 | tf_op jit(solution)/shard_map/pallas_call | solution.py:451
  42.5 11.1 %shard_map.96 = (bf16[2,3,128,256]{3,2,1,0:T(8,128)(2,1)}, bf16[2,3,128,256]{3,2,1,0:T(8,128)(2,1)}, bf16[2,3,128,256]{3,2,1,0:T(8,128)(2,1)}, bf16[2,3,128,256]{3,2,1,0:T(8,128)(2,1)}, f32[8,128]{1,0:T(8,128)}) custom-call(s32[14]{0:T(128)} %pad_add_fusion.scalars_ref, bf16[4,128,256]{2,1,0:T(8,128)(2,1)} %get-tuple-element.71.refs_0_, ...), custom_call_target="tpu_custom_call" | custom-call | flops 16499999744 | bytes 65536 | tf_op jit(solution)/shard_map/pallas_call | solution.py:475
  54.0 2.4 %collective-permute-start.11 = (bf16[2,3,128,256]{3,2,1,0:T(8,128)(2,1)}, bf16[2,3,128,256]{3,2,1,0:T(8,128)(2,1)S(1)}, u32[]{:S(2)}, u32[]{:S(2)}) collective-permute-start(bf16[2,3,128,256]{3,2,1,0:T(8,128)(2,1)} %get-tuple-element.87), channel_id=1, source_target_pairs={{0,4},{1,5},{2,6},{3,7},{4,0},{5,1},{6,2},{7,3},{8,12},{9,13},{10,... | collective-permute-start | bytes 1179656 | tf_op jit(solution)/shard_map/ppermute | solution.py:46
  57.9 9.3 %shard_map.97 = (bf16[16,8,2,16,128]{4,3,2,1,0:T(8,128)(2,1)}, bf16[2,4,3,256,256]{4,3,2,1,0:T(8,128)(2,1)}, bf16[2,4,3,256,256]{4,3,2,1,0:T(8,128)(2,1)}, f32[8,128]{1,0:T(8,128)}) custom-call(s32[14]{0:T(128)} %pad_add_fusion.scalars_ref, bf16[2,4,128,256]{3,2,1,0:T(8,128)(2,1)} %get-tuple-element.67.refs_0_.refs_4_, ...), custom_call_target="tpu_custom_call", output_to_operand_aliasing={{0}: (9, {})} | custom-call | flops 11000000512 | bytes 65536 | tf_op jit(solution)/shard_map/pallas_call | solution.py:451
  67.3 15.3 %all-to-all-start = ((bf16[256,16,128]{2,1,0:T(8,128)(2,1)}), bf16[256,16,128]{2,1,0:T(8,128)(2,1)S(1)}, u32[]{:S(2)}, u32[]{:S(2)}) async-start(bf16[256,16,128]{2,1,0:T(8,128)(2,1)} %bitcast.18), calls=%async_computation | async-start | bytes 2097152 | tf_op jit(solution)/shard_map/all_to_all | solution.py:552
  82.6 11.1 %shard_map.98 = (bf16[3,128,256]{2,1,0:T(8,128)(2,1)}, bf16[3,128,256]{2,1,0:T(8,128)(2,1)}, bf16[3,128,256]{2,1,0:T(8,128)(2,1)}, bf16[3,128,256]{2,1,0:T(8,128...) custom-call(s32[14]{0:T(128)} %pad_add_fusion.scalars_ref, ...), custom_call_target="tpu_custom_call" | custom-call | flops 16499999744 | bytes 65536 | tf_op jit(solution)/shard_map/pallas_call | solution.py:475
  94.6 2.0 %shard_map.100 = (bf16[5,3,128,256]{3,2,1,0:T(8,128)(2,1)}, f32[8,128]{1,0:T(8,128)}) custom-call(bf16[2,3,128,256]{3,2,1,0:T(8,128)(2,1)} %get-tuple-element.85.refs_0_, bf16[2,3,128,256]{3,2,1,0:T(8,128)(2,1)} %copy-done.4, bf16[2,3,128,256]{3,2,1,0:T(8,128)(2,1)} %copy-done.5, bf16[2,3,128,256]{3,2,1,0:T(8,128)(2,1)} %collective-permute-done.12.refs_11_.refs_3_, ...), custom_call_target="tpu_custom_call" | custom-call | flops 55000000 | bytes 65536 | tf_op jit(solution)/shard_map/pallas_call | solution.py:103
  99.4 2.9 %shard_map.101 = (bf16[16,1,16,16,128]{4,3,2,1,0:T(8,128)(2,1)}, f32[8,128]{1,0:T(8,128)}) custom-call(s32[16]{0:T(128)} %broadcast_clamp_fusion.sender_ref, bf16[16,16,16,128]{3,2,1,0:T(8,128)(2,1)} %bitcast.17, f32[8,128]{1,0:T(8,128)} %get-tuple-element.102.refs_1_), custom_call_target="tpu_custom_call" | custom-call | flops 55000000 | bytes 65536 | tf_op jit(solution)/shard_map/pallas_call | solution.py:249
  102.2 8.2 %all-to-all-start.1 = ((bf16[16,1,16,16,128]{4,3,2,1,0:T(8,128)(2,1)}), bf16[16,1,16,16,128]{4,3,2,1,0:T(8,128)(2,1)S(1)}, u32[]{:S(2)}, u32[]{:S(2)}) async-start(bf16[16,1,16,16,128]{4,3,2,1,0:T(8,128)(2,1)} %get-tuple-element.103), calls=%async_computation.1 | async-start | bytes 2097152 | tf_op jit(solution)/shard_map/all_to_all | solution.py:564
  110.6 2.1 %collective-permute-start.15 = (bf16[3,128,256]{2,1,0:T(8,128)(2,1)}, bf16[3,128,256]{2,1,0:T(8,128)(2,1)S(1)}, u32[]{:S(2)}, u32[]{:S(2)}) collective-permute-start(bf16[3,128,256]{2,1,0:T(8,128)(2,1)} %get-tuple-element.107), channel_id=1, source_target_pairs={{0,3},{1,2},{2,5},{3,4},{4,7},{5,6},{6,1},{7,0},{8,11},{9,10},{10,... | collective-permute-start | bytes 589832 | tf_op jit(solution)/shard_map/ppermute | solution.py:55
  114.0 2.4 %collective-permute-done.14.refs_6_.refs_2_ = bf16[3,128,256]{2,1,0:T(8,128)(2,1)S(1)} collective-permute-done((bf16[3,128,256]{2,1,0:T(8,128)(2,1)}, bf16[3,128,256]{2,1,0:T(8,128)(2,1)S(1)}, u32[]{:S(2)}, u32[]{:S(2)}) %collective-permute-start.14) | collective-permute-done | bytes 196640 | tf_op jit(solution)/shard_map/ppermute | solution.py:46
  117.5 5.6 %collective-permute-done.15.refs_7_.refs_3_ = bf16[3,128,256]{2,1,0:T(8,128)(2,1)S(1)} collective-permute-done((bf16[3,128,256]{2,1,0:T(8,128)(2,1)}, bf16[3,128,256]{2,1,0:T(8,128)(2,1)S(1)}, u32[]{:S(2)}, u32[]{:S(2)}) %collective-permute-start.15) | collective-permute-done | bytes 196640 | tf_op jit(solution)/shard_map/ppermute | solution.py:55
  123.1 10.5 %collective-permute-done.17.refs_9_.refs_5_ = bf16[3,128,256]{2,1,0:T(8,128)(2,1)S(1)} collective-permute-done((bf16[3,128,256]{2,1,0:T(8,128)(2,1)}, bf16[3,128,256]{2,1,0:T(8,128)(2,1)S(1)}, u32[]{:S(2)}, u32[]{:S(2)}) %collective-permute-start.17) | collective-permute-done | bytes 196640 | tf_op jit(solution)/shard_map/ppermute | solution.py:55
  134.3 2.4 %shard_map.102 = (bf16[128,4096]{1,0:T(8,128)(2,1)}, bf16[128,4096]{1,0:T(8,128)(2,1)}, bf16[128,4096]{1,0:T(8,128)(2,1)}, f32[8,128]{1,0:T(8,128)}) custom-call(bf16[2,3,128,256]{3,2,1,0:T(8,128)(2,1)} %get-tuple-element.85.refs_0_, bf16[5,3,128,256]{3,2,1,0:T(8,128)(2,1)} %collective-permute-done.13.refs_1_, bf16[2,3,128,256]{3,2,1,0:T(8,128)(2,1)} %copy-done.4, ...), custom_call_target="tpu_custom_call" | custom-call | flops 55000000 | bytes 65536 | tf_op jit(solution)/shard_map/pallas_call | solution.py:215
  136.7 2.2 %shard_map.103 = (bf16[128,4096]{1,0:T(8,128)(2,1)}, bf16[128,4096]{1,0:T(8,128)(2,1)}, bf16[128,4096]{1,0:T(8,128)(2,1)}, f32[8,128]{1,0:T(8,128)}) custom-call(bf16[3,128,256]{2,1,0:T(8,128)(2,1)} %get-tuple-element.104.refs_0_, ...), custom_call_target="tpu_custom_call", output_to_operand_aliasing={{0}: (6, {}), {1}: (7, {}), {2}: (8, {})} | custom-call | flops 55000000 | bytes 65536 | tf_op jit(solution)/shard_map/pallas_call | solution.py:215
  140.0 2.1 %shard_map.104 = (bf16[128,4096]{1,0:T(8,128)(2,1)}, f32[8,128]{1,0:T(8,128)}) custom-call(bf16[2,8,8,2,16,128]{5,4,3,2,1,0:T(8,128)(2,1)} %bitcast.16, f32[8,128]{1,0:T(8,128)} %get-tuple-element.115.refs_0_), custom_call_target="tpu_custom_call" | custom-call | flops 55000000 | bytes 65536 | tf_op jit(solution)/shard_map/pallas_call | solution.py:285
  (74 shorter events, 15.0 us)
Async XLA Ops:
  0.6 20.8 %copy-start.14 = (s32[16]{0:T(128)S(1)}, s32[16]{0:T(128)}, u32[]{:S(2)}) copy-start(s32[16]{0:T(128)} %param.11) | copy-start | bytes 196
  4.6 15.4 %collective-permute-start = (bf16[5,4,128,256]{3,2,1,0:T(8,128)(2,1)}, bf16[5,4,128,256]{3,2,1,0:T(8,128)(2,1)S(1)}, u32[]{:S(2)}, u32[]{:S(2)}) collective-permute-start(bf16[5,4,128,256]{3,2,1,0:T(8,128)(2,1)} %get-tuple-element.65), channel_id=1, source_target_pairs={{0,1},{1,0},{2,3},{3,2},{4,5},{5,4},{6,7},{7,6},{8,9},{9,8},{10,11... | collective-permute-start | bytes 3932168 | tf_op jit(solution)/shard_map/ppermute | solution.py:50
  5.4 8.1 %collective-permute-start.4 = (bf16[4,128,256]{2,1,0:T(8,128)(2,1)}, bf16[4,128,256]{2,1,0:T(8,128)(2,1)S(1)}, u32[]{:S(2)}, u32[]{:S(2)}) collective-permute-start(bf16[4,128,256]{2,1,0:T(8,128)(2,1)} %get-tuple-element.72), channel_id=1, source_target_pairs={{0,2},{1,3},{2,4},{3,5},{4,6},{5,7},{6,0},{7,1},{8,10},{9,11},{10,... | collective-permute-start | bytes 786440 | tf_op jit(solution)/shard_map/ppermute | solution.py:46
  5.4 18.9 %collective-permute-start.5 = (bf16[4,128,256]{2,1,0:T(8,128)(2,1)}, bf16[4,128,256]{2,1,0:T(8,128)(2,1)S(1)}, u32[]{:S(2)}, u32[]{:S(2)}) collective-permute-start(bf16[4,128,256]{2,1,0:T(8,128)(2,1)} %get-tuple-element.73), channel_id=1, source_target_pairs={{0,4},{1,5},{2,6},{3,7},{4,0},{5,1},{6,2},{7,3},{8,12},{9,13},{10,... | collective-permute-start | bytes 786440 | tf_op jit(solution)/shard_map/ppermute | solution.py:46
  7.6 19.3 %collective-permute-start.6 = (bf16[4,128,256]{2,1,0:T(8,128)(2,1)}, bf16[4,128,256]{2,1,0:T(8,128)(2,1)}, u32[]{:S(2)}, u32[]{:S(2)}) collective-permute-start(bf16[4,128,256]{2,1,0:T(8,128)(2,1)} %get-tuple-element.74), channel_id=1, source_target_pairs={{0,6},{1,7},{2,0},{3,1},{4,2},{5,3},{6,4},{7,5},{8,14},{9,15},{10,... | collective-permute-start | bytes 786440 | tf_op jit(solution)/shard_map/ppermute | solution.py:46
  7.6 19.3 %collective-permute-start.7 = (bf16[4,128,256]{2,1,0:T(8,128)(2,1)}, bf16[4,128,256]{2,1,0:T(8,128)(2,1)}, u32[]{:S(2)}, u32[]{:S(2)}) collective-permute-start(bf16[4,128,256]{2,1,0:T(8,128)(2,1)} %get-tuple-element.75), channel_id=1, source_target_pairs={{0,3},{1,2},{2,5},{3,4},{4,7},{5,6},{6,1},{7,0},{8,11},{9,10},{10,... | collective-permute-start | bytes 786440 | tf_op jit(solution)/shard_map/ppermute | solution.py:55
  13.5 19.7 %copy-start.10 = (bf16[4,128,256]{2,1,0:T(8,128)(2,1)}, bf16[4,128,256]{2,1,0:T(8,128)(2,1)S(1)}, u32[]{:S(2)}) copy-start(bf16[4,128,256]{2,1,0:T(8,128)(2,1)S(1)} %collective-permute-done.4.refs_1_) | copy-start | bytes 786436
  13.5 14.2 %collective-permute-start.8 = (bf16[4,128,256]{2,1,0:T(8,128)(2,1)}, bf16[4,128,256]{2,1,0:T(8,128)(2,1)}, u32[]{:S(2)}, u32[]{:S(2)}) collective-permute-start(bf16[4,128,256]{2,1,0:T(8,128)(2,1)} %get-tuple-element.76), channel_id=1, source_target_pairs={{0,5},{1,4},{2,7},{3,6},{4,1},{5,0},{6,3},{7,2},{8,13},{9,12},{10,... | collective-permute-start | bytes 786440 | tf_op jit(solution)/shard_map/ppermute | solution.py:55
  20.0 13.1 %collective-permute-start.9 = (bf16[4,128,256]{2,1,0:T(8,128)(2,1)}, bf16[4,128,256]{2,1,0:T(8,128)(2,1)}, u32[]{:S(2)}, u32[]{:S(2)}) collective-permute-start(bf16[4,128,256]{2,1,0:T(8,128)(2,1)} %get-tuple-element.77), channel_id=1, source_target_pairs={{0,7},{1,6},{2,1},{3,0},{4,3},{5,2},{6,5},{7,4},{8,15},{9,14},{10,... | collective-permute-start | bytes 786440 | tf_op jit(solution)/shard_map/ppermute | solution.py:55
  24.3 32.1 %collective-permute-start.1 = (bf16[2,4,128,256]{3,2,1,0:T(8,128)(2,1)}, bf16[2,4,128,256]{3,2,1,0:T(8,128)(2,1)S(1)}, u32[]{:S(2)}, u32[]{:S(2)}) collective-permute-start(bf16[2,4,128,256]{3,2,1,0:T(8,128)(2,1)} %get-tuple-element.68), channel_id=1, source_target_pairs={{0,2},{1,3},{2,4},{3,5},{4,6},{5,7},{6,0},{7,1},{8,10},{9,11},{10,... | collective-permute-start | bytes 1572872 | tf_op jit(solution)/shard_map/ppermute | solution.py:46
  27.0 30.2 %collective-permute-start.2 = (bf16[2,4,128,256]{3,2,1,0:T(8,128)(2,1)}, bf16[2,4,128,256]{3,2,1,0:T(8,128)(2,1)S(1)}, u32[]{:S(2)}, u32[]{:S(2)}) collective-permute-start(bf16[2,4,128,256]{3,2,1,0:T(8,128)(2,1)} %get-tuple-element.69), channel_id=1, source_target_pairs={{0,4},{1,5},{2,6},{3,7},{4,0},{5,1},{6,2},{7,3},{8,12},{9,13},{10,... | collective-permute-start | bytes 1572872 | tf_op jit(solution)/shard_map/ppermute | solution.py:46
  27.0 30.2 %collective-permute-start.3 = (bf16[2,4,128,256]{3,2,1,0:T(8,128)(2,1)}, bf16[2,4,128,256]{3,2,1,0:T(8,128)(2,1)}, u32[]{:S(2)}, u32[]{:S(2)}) collective-permute-start(bf16[2,4,128,256]{3,2,1,0:T(8,128)(2,1)} %get-tuple-element.70), channel_id=1, source_target_pairs={{0,6},{1,7},{2,0},{3,1},{4,2},{5,3},{6,4},{7,5},{8,14},{9,15},{10,... | collective-permute-start | bytes 1572872 | tf_op jit(solution)/shard_map/ppermute | solution.py:46
  53.5 40.1 %collective-permute-start.10 = (bf16[2,3,128,256]{3,2,1,0:T(8,128)(2,1)}, bf16[2,3,128,256]{3,2,1,0:T(8,128)(2,1)S(1)}, u32[]{:S(2)}, u32[]{:S(2)}) collective-permute-start(bf16[2,3,128,256]{3,2,1,0:T(8,128)(2,1)} %get-tuple-element.86), channel_id=1, source_target_pairs={{0,2},{1,3},{2,4},{3,5},{4,6},{5,7},{6,0},{7,1},{8,10},{9,11},{10,... | collective-permute-start | bytes 1179656 | tf_op jit(solution)/shard_map/ppermute | solution.py:46
  54.0 39.8 %collective-permute-start.11 = (bf16[2,3,128,256]{3,2,1,0:T(8,128)(2,1)}, bf16[2,3,128,256]{3,2,1,0:T(8,128)(2,1)S(1)}, u32[]{:S(2)}, u32[]{:S(2)}) collective-permute-start(bf16[2,3,128,256]{3,2,1,0:T(8,128)(2,1)} %get-tuple-element.87), channel_id=1, source_target_pairs={{0,4},{1,5},{2,6},{3,7},{4,0},{5,1},{6,2},{7,3},{8,12},{9,13},{10,... | collective-permute-start | bytes 1179656 | tf_op jit(solution)/shard_map/ppermute | solution.py:46
  56.4 37.4 %collective-permute-start.12 = (bf16[2,3,128,256]{3,2,1,0:T(8,128)(2,1)}, bf16[2,3,128,256]{3,2,1,0:T(8,128)(2,1)}, u32[]{:S(2)}, u32[]{:S(2)}) collective-permute-start(bf16[2,3,128,256]{3,2,1,0:T(8,128)(2,1)} %get-tuple-element.88), channel_id=1, source_target_pairs={{0,6},{1,7},{2,0},{3,1},{4,2},{5,3},{6,4},{7,5},{8,14},{9,15},{10,... | collective-permute-start | bytes 1179656 | tf_op jit(solution)/shard_map/ppermute | solution.py:46
  67.3 31.1 %all-to-all-start = ((bf16[256,16,128]{2,1,0:T(8,128)(2,1)}), bf16[256,16,128]{2,1,0:T(8,128)(2,1)S(1)}, u32[]{:S(2)}, u32[]{:S(2)}) async-start(bf16[256,16,128]{2,1,0:T(8,128)(2,1)} %bitcast.18), calls=%async_computation | async-start | bytes 2097152 | tf_op jit(solution)/shard_map/all_to_all | solution.py:552
  96.6 37.0 %collective-permute-start.13 = (bf16[5,3,128,256]{3,2,1,0:T(8,128)(2,1)}, bf16[5,3,128,256]{3,2,1,0:T(8,128)(2,1)}, u32[]{:S(2)}, u32[]{:S(2)}) collective-permute-start(bf16[5,3,128,256]{3,2,1,0:T(8,128)(2,1)} %get-tuple-element.105), channel_id=1, source_target_pairs={{0,1},{1,0},{2,3},{3,2},{4,5},{5,4},{6,7},{7,6},{8,9},{9,8},{10,11... | collective-permute-start | bytes 2949128 | tf_op jit(solution)/shard_map/ppermute | solution.py:50
  102.2 36.7 %all-to-all-start.1 = ((bf16[16,1,16,16,128]{4,3,2,1,0:T(8,128)(2,1)}), bf16[16,1,16,16,128]{4,3,2,1,0:T(8,128)(2,1)S(1)}, u32[]{:S(2)}, u32[]{:S(2)}) async-start(bf16[16,1,16,16,128]{4,3,2,1,0:T(8,128)(2,1)} %get-tuple-element.103), calls=%async_computation.1 | async-start | bytes 2097152 | tf_op jit(solution)/shard_map/all_to_all | solution.py:564
  110.5 5.9 %collective-permute-start.14 = (bf16[3,128,256]{2,1,0:T(8,128)(2,1)}, bf16[3,128,256]{2,1,0:T(8,128)(2,1)S(1)}, u32[]{:S(2)}, u32[]{:S(2)}) collective-permute-start(bf16[3,128,256]{2,1,0:T(8,128)(2,1)} %get-tuple-element.106), channel_id=1, source_target_pairs={{0,2},{1,3},{2,4},{3,5},{4,6},{5,7},{6,0},{7,1},{8,10},{9,11},{10,... | collective-permute-start | bytes 589832 | tf_op jit(solution)/shard_map/ppermute | solution.py:46
  110.6 12.5 %collective-permute-start.15 = (bf16[3,128,256]{2,1,0:T(8,128)(2,1)}, bf16[3,128,256]{2,1,0:T(8,128)(2,1)S(1)}, u32[]{:S(2)}, u32[]{:S(2)}) collective-permute-start(bf16[3,128,256]{2,1,0:T(8,128)(2,1)} %get-tuple-element.107), channel_id=1, source_target_pairs={{0,3},{1,2},{2,5},{3,4},{4,7},{5,6},{6,1},{7,0},{8,11},{9,10},{10,... | collective-permute-start | bytes 589832 | tf_op jit(solution)/shard_map/ppermute | solution.py:55
  112.7 10.4 %collective-permute-start.16 = (bf16[3,128,256]{2,1,0:T(8,128)(2,1)}, bf16[3,128,256]{2,1,0:T(8,128)(2,1)S(1)}, u32[]{:S(2)}, u32[]{:S(2)}) collective-permute-start(bf16[3,128,256]{2,1,0:T(8,128)(2,1)} %get-tuple-element.108), channel_id=1, source_target_pairs={{0,6},{1,7},{2,0},{3,1},{4,2},{5,3},{6,4},{7,5},{8,14},{9,15},{10,... | collective-permute-start | bytes 589832 | tf_op jit(solution)/shard_map/ppermute | solution.py:46
  112.9 20.7 %collective-permute-start.17 = (bf16[3,128,256]{2,1,0:T(8,128)(2,1)}, bf16[3,128,256]{2,1,0:T(8,128)(2,1)S(1)}, u32[]{:S(2)}, u32[]{:S(2)}) collective-permute-start(bf16[3,128,256]{2,1,0:T(8,128)(2,1)} %get-tuple-element.109), channel_id=1, source_target_pairs={{0,7},{1,6},{2,1},{3,0},{4,3},{5,2},{6,5},{7,4},{8,15},{9,14},{10,... | collective-permute-start | bytes 589832 | tf_op jit(solution)/shard_map/ppermute | solution.py:55
  116.4 25.7 %collective-permute-start.18 = (bf16[3,128,256]{2,1,0:T(8,128)(2,1)}, bf16[3,128,256]{2,1,0:T(8,128)(2,1)}, u32[]{:S(2)}, u32[]{:S(2)}) collective-permute-start(bf16[3,128,256]{2,1,0:T(8,128)(2,1)} %get-tuple-element.117), channel_id=1, source_target_pairs={{0,4},{1,5},{2,6},{3,7},{4,0},{5,1},{6,2},{7,3},{8,12},{9,13},{10,... | collective-permute-start | bytes 589832 | tf_op jit(solution)/shard_map/ppermute | solution.py:46
  123.0 19.0 %collective-permute-start.19 = (bf16[3,128,256]{2,1,0:T(8,128)(2,1)}, bf16[3,128,256]{2,1,0:T(8,128)(2,1)}, u32[]{:S(2)}, u32[]{:S(2)}) collective-permute-start(bf16[3,128,256]{2,1,0:T(8,128)(2,1)} %get-tuple-element.118), channel_id=1, source_target_pairs={{0,5},{1,4},{2,7},{3,6},{4,1},{5,0},{6,3},{7,2},{8,13},{9,12},{10,... | collective-permute-start | bytes 589832 | tf_op jit(solution)/shard_map/ppermute | solution.py:55
  (13 other events, 65.1 us)

commit v3 on v1

--- a/solution.py
+++ b/solution.py
@@ -566,9 +566,8 @@
     landed = lax.all_to_all(slots, "dp", split_axis=0, concat_axis=0, tiled=True)
     landed = landed.reshape(groups, PEERS, CHUNKS, 16, HEAD_DIM)
 
-    near = [own[1], sib[1], own[3], sib[3]]
     grads, token = unpack(
-        [(x, 0) for x in got], [(other, d) for d in range(CHIPS)], None, 0, token + near
+        [(x, 0) for x in got], [(other, d) for d in range(CHIPS)], None, 0, token
     )
     grads, token = unpack(
         [(x, None) for x in own], [(other, CHIPS)] + [(x, None) for x in sib[1:]], grads, 1, token

time: 141 us -> 140 us (level)
  starting transfers between devices: 49.9 us -> 53.6 us
  waiting for transfers between devices: 16 us -> 13 us
    ppermute x6, starting transfers between devices: 15.9 us -> 18.9 us  [turn_across(): return lax.ppermute(x, 'seq', pairs)]
    ppermute x6, waiting for transfers between devices: 9.78 us -> 7.88 us  [turn_across(): return lax.ppermute(x, 'seq', pairs)]
  transfers between devices with their start and end apart: 22 -> 22, of which waited for: 8 -> 5; matrix products, arithmetic and copies ran while one was open for 1% -> 1% of each run, Pallas kernels for 43% -> 43%
where the time goes in v3:
time: 140 us; the launch traced here: 139 us
  Pallas kernels  65.9 us (47%)
  starting transfers between devices  53.6 us (38%)
  waiting for transfers between devices  13 us (9%)
  local copies, waits for them, and re-layouts  3.97 us (3%)
  other arithmetic  1.76 us (1%)
    pallas_call x2, Pallas kernels, backward(): pl.pallas_call(functools.partial(backward_kernel, by_chip), out_shape=[ja...  25.9 us
    pallas_call x2, Pallas kernels, forward(): pl.pallas_call(forward_kernel, out_shape=[jax.ShapeDtypeStruct(out, jnp.b...  21.5 us
    ppermute x6, starting transfers between devices, turn_across(): return lax.ppermute(x, 'seq', pairs)  18.9 us
    ppermute x12, starting transfers between devices, turn(): return lax.ppermute(x, 'seq', pairs)  18.1 us
    all_to_all x1, starting transfers between devices, local(): lax.all_to_all(out.reshape(groups * PEERS * CHUNKS, 16, HEAD_DIM), ('dp',...  8.79 us
    pallas_call x3, Pallas kernels, copy_kernel(): pl.pallas_call(kernel, out_shape=[jax.ShapeDtypeStruct(x, jnp.bfloat16) f...  8.68 us
    ppermute x6, waiting for transfers between devices, turn_across(): return lax.ppermute(x, 'seq', pairs)  7.88 us
    all_to_all x1, starting transfers between devices, local(): lax.all_to_all(slots, 'dp', split_axis=0, concat_axis=0, tiled=True)  5.09 us
  transfers between devices with their start and end apart: 22, of which 5 were waited for; matrix products, arithmetic and copies ran while one was open for 1% of the time, Pallas kernels for 43%

profile of v3, /device:TPU:1, one launch (start us, length us, event | category | flops | bytes accessed | tf_op | source)
XLA Modules:
  0.0 139.2 jit_solution(15985372735166523290)
XLA Ops:
  0.7 4.0 %shard_map.93 = (bf16[4,128,256]{2,1,0:T(8,128)(2,1)}, bf16[4,128,256]{2,1,0:T(8,128)(2,1)}, bf16[4,128,256]{2,1,0:T(8,128)(2,1)}, bf16[4,128,256]{2,1,0:T(8,128...) custom-call(bf16[128,4096]{1,0:T(8,128)(2,1)} %refs_0_.3, ...), custom_call_target="tpu_custom_call" | custom-call | flops 55000000 | bytes 65536 | tf_op jit(solution)/shard_map/pallas_call | solution.py:103
  4.6 1.5 %collective-permute-start = (bf16[5,4,128,256]{3,2,1,0:T(8,128)(2,1)}, bf16[5,4,128,256]{3,2,1,0:T(8,128)(2,1)S(1)}, u32[]{:S(2)}, u32[]{:S(2)}) collective-permute-start(bf16[5,4,128,256]{3,2,1,0:T(8,128)(2,1)} %get-tuple-element.61), channel_id=1, source_target_pairs={{0,1},{1,0},{2,3},{3,2},{4,5},{5,4},{6,7},{7,6},{8,9},{9,8},{10,11... | collective-permute-start | bytes 3932168 | tf_op jit(solution)/shard_map/ppermute | solution.py:50
  7.5 2.6 %collective-permute-start.5 = (bf16[4,128,256]{2,1,0:T(8,128)(2,1)}, bf16[4,128,256]{2,1,0:T(8,128)(2,1)S(1)}, u32[]{:S(2)}, u32[]{:S(2)}) collective-permute-start(bf16[4,128,256]{2,1,0:T(8,128)(2,1)} %get-tuple-element.69), channel_id=1, source_target_pairs={{0,4},{1,5},{2,6},{3,7},{4,0},{5,1},{6,2},{7,3},{8,12},{9,13},{10,... | collective-permute-start | bytes 786440 | tf_op jit(solution)/shard_map/ppermute | solution.py:46
  13.0 2.8 %collective-permute-done.4.refs_1_ = bf16[4,128,256]{2,1,0:T(8,128)(2,1)S(1)} collective-permute-done((bf16[4,128,256]{2,1,0:T(8,128)(2,1)}, bf16[4,128,256]{2,1,0:T(8,128)(2,1)S(1)}, u32[]{:S(2)}, u32[]{:S(2)}) %collective-permute-start.4) | collective-permute-done | bytes 262176 | tf_op jit(solution)/shard_map/ppermute | solution.py:46
  15.7 8.3 %collective-permute-start.8 = (bf16[4,128,256]{2,1,0:T(8,128)(2,1)}, bf16[4,128,256]{2,1,0:T(8,128)(2,1)}, u32[]{:S(2)}, u32[]{:S(2)}) collective-permute-start(bf16[4,128,256]{2,1,0:T(8,128)(2,1)} %get-tuple-element.72), channel_id=1, source_target_pairs={{0,5},{1,4},{2,7},{3,6},{4,1},{5,0},{6,3},{7,2},{8,13},{9,12},{10,... | collective-permute-start | bytes 786440 | tf_op jit(solution)/shard_map/ppermute | solution.py:55
  25.1 2.7 %shard_map.94 = (bf16[2,4,128,256]{3,2,1,0:T(8,128)(2,1)}, bf16[2,4,128,256]{3,2,1,0:T(8,128)(2,1)}, bf16[2,4,128,256]{3,2,1,0:T(8,128)(2,1)}, bf16[2,4,128,256]{3,2,1,0:T(8,128)(2,1)}, f32[8,128]{1,0:T(8,128)}) custom-call(bf16[128,4096]{1,0:T(8,128)(2,1)} %refs_0_.3, bf16[128,4096]{1,0:T(8,128)(2,1)} %refs_1_.3, bf16[128,4096]{1,0:T(8,128)(2,1)} %refs_2_.3, ...), custom_call_target="tpu_custom_call" | custom-call | flops 55000000 | bytes 65536 | tf_op jit(solution)/shard_map/pallas_call | solution.py:103
  30.6 3.8 %collective-permute-done.8.refs_6_ = bf16[4,128,256]{2,1,0:T(8,128)(2,1)} collective-permute-done((bf16[4,128,256]{2,1,0:T(8,128)(2,1)}, bf16[4,128,256]{2,1,0:T(8,128)(2,1)}, u32[]{:S(2)}, u32[]{:S(2)}) %collective-permute-start.8) | collective-permute-done | bytes 262176 | tf_op jit(solution)/shard_map/ppermute | solution.py:55
  34.4 10.8 %shard_map.95 = (bf16[16,8,2,16,128]{4,3,2,1,0:T(8,128)(2,1)}, bf16[2,4,3,256,256]{4,3,2,1,0:T(8,128)(2,1)}, bf16[2,4,3,256,256]{4,3,2,1,0:T(8,128)(2,1)}, f32[8,128]{1,0:T(8,128)}) custom-call(s32[14]{0:T(128)} %pad_add_fusion.scalars_ref, bf16[4,128,256]{2,1,0:T(8,128)(2,1)} %get-tuple-element.67.refs_0_, bf16[4,128,256]{2,1,0:T(8,128)(2,1)} %copy-done.6, ...), custom_call_target="tpu_custom_call" | custom-call | flops 55000000 | bytes 65536 | tf_op jit(solution)/shard_map/pallas_call | solution.py:453
  45.2 12.9 %shard_map.96 = (bf16[2,3,128,256]{3,2,1,0:T(8,128)(2,1)}, bf16[2,3,128,256]{3,2,1,0:T(8,128)(2,1)}, bf16[2,3,128,256]{3,2,1,0:T(8,128)(2,1)}, bf16[2,3,128,256]{3,2,1,0:T(8,128)(2,1)}, f32[8,128]{1,0:T(8,128)}) custom-call(s32[14]{0:T(128)} %pad_add_fusion.scalars_ref, bf16[4,128,256]{2,1,0:T(8,128)(2,1)} %get-tuple-element.67.refs_0_, ...), custom_call_target="tpu_custom_call" | custom-call | flops 16499999744 | bytes 65536 | tf_op jit(solution)/shard_map/pallas_call | solution.py:477
  58.1 2.6 %collective-permute-start.10 = (bf16[2,3,128,256]{3,2,1,0:T(8,128)(2,1)}, bf16[2,3,128,256]{3,2,1,0:T(8,128)(2,1)S(1)}, u32[]{:S(2)}, u32[]{:S(2)}) collective-permute-start(bf16[2,3,128,256]{3,2,1,0:T(8,128)(2,1)} %get-tuple-element.82), channel_id=1, source_target_pairs={{0,2},{1,3},{2,4},{3,5},{4,6},{5,7},{6,0},{7,1},{8,10},{9,11},{10,... | collective-permute-start | bytes 1179656 | tf_op jit(solution)/shard_map/ppermute | solution.py:46
  61.6 1.6 %collective-permute-start.12 = (bf16[2,3,128,256]{3,2,1,0:T(8,128)(2,1)}, bf16[2,3,128,256]{3,2,1,0:T(8,128)(2,1)}, u32[]{:S(2)}, u32[]{:S(2)}) collective-permute-start(bf16[2,3,128,256]{3,2,1,0:T(8,128)(2,1)} %get-tuple-element.84), channel_id=1, source_target_pairs={{0,6},{1,7},{2,0},{3,1},{4,2},{5,3},{6,4},{7,5},{8,14},{9,15},{10,... | collective-permute-start | bytes 1179656 | tf_op jit(solution)/shard_map/ppermute | solution.py:46
  64.0 10.8 %shard_map.97 = (bf16[16,8,2,16,128]{4,3,2,1,0:T(8,128)(2,1)}, bf16[2,4,3,256,256]{4,3,2,1,0:T(8,128)(2,1)}, bf16[2,4,3,256,256]{4,3,2,1,0:T(8,128)(2,1)}, f32[8,128]{1,0:T(8,128)}) custom-call(s32[14]{0:T(128)} %pad_add_fusion.scalars_ref, bf16[2,4,128,256]{3,2,1,0:T(8,128)(2,1)} %get-tuple-element.63.refs_0_.refs_4_, ...), custom_call_target="tpu_custom_call", output_to_operand_aliasing={{0}: (9, {})} | custom-call | flops 11000000512 | bytes 65536 | tf_op jit(solution)/shard_map/pallas_call | solution.py:453
  74.7 8.8 %all-to-all-start = ((bf16[256,16,128]{2,1,0:T(8,128)(2,1)}), bf16[256,16,128]{2,1,0:T(8,128)(2,1)S(1)}, u32[]{:S(2)}, u32[]{:S(2)}) async-start(bf16[256,16,128]{2,1,0:T(8,128)(2,1)} %bitcast.18), calls=%async_computation | async-start | bytes 2097152 | tf_op jit(solution)/shard_map/all_to_all | solution.py:554
  83.5 13.0 %shard_map.98 = (bf16[3,128,256]{2,1,0:T(8,128)(2,1)}, bf16[3,128,256]{2,1,0:T(8,128)(2,1)}, bf16[3,128,256]{2,1,0:T(8,128)(2,1)}, bf16[3,128,256]{2,1,0:T(8,128...) custom-call(s32[14]{0:T(128)} %pad_add_fusion.scalars_ref, ...), custom_call_target="tpu_custom_call" | custom-call | flops 16499999744 | bytes 65536 | tf_op jit(solution)/shard_map/pallas_call | solution.py:477
  97.4 2.0 %shard_map.100 = (bf16[5,3,128,256]{3,2,1,0:T(8,128)(2,1)}, f32[8,128]{1,0:T(8,128)}) custom-call(bf16[2,3,128,256]{3,2,1,0:T(8,128)(2,1)} %get-tuple-element.81.refs_0_, bf16[2,3,128,256]{3,2,1,0:T(8,128)(2,1)} %copy-done.4, bf16[2,3,128,256]{3,2,1,0:T(8,128)(2,1)} %copy-done.5, bf16[2,3,128,256]{3,2,1,0:T(8,128)(2,1)} %collective-permute-done.12.refs_11_.refs_3_, ...), custom_call_target="tpu_custom_call" | custom-call | flops 55000000 | bytes 65536 | tf_op jit(solution)/shard_map/pallas_call | solution.py:103
  103.4 2.9 %shard_map.101 = (bf16[16,1,16,16,128]{4,3,2,1,0:T(8,128)(2,1)}, f32[8,128]{1,0:T(8,128)}) custom-call(s32[16]{0:T(128)} %broadcast_clamp_fusion.sender_ref, bf16[16,16,16,128]{3,2,1,0:T(8,128)(2,1)} %bitcast.17, f32[8,128]{1,0:T(8,128)} %get-tuple-element.98.refs_1_), custom_call_target="tpu_custom_call" | custom-call | flops 55000000 | bytes 65536 | tf_op jit(solution)/shard_map/pallas_call | solution.py:251
  106.3 5.1 %all-to-all-start.1 = ((bf16[16,1,16,16,128]{4,3,2,1,0:T(8,128)(2,1)}), bf16[16,1,16,16,128]{4,3,2,1,0:T(8,128)(2,1)S(1)}, u32[]{:S(2)}, u32[]{:S(2)}) async-start(bf16[16,1,16,16,128]{4,3,2,1,0:T(8,128)(2,1)} %get-tuple-element.99), calls=%async_computation.1 | async-start | bytes 2097152 | tf_op jit(solution)/shard_map/all_to_all | solution.py:566
  112.9 2.5 %collective-permute-start.14 = (bf16[3,128,256]{2,1,0:T(8,128)(2,1)}, bf16[3,128,256]{2,1,0:T(8,128)(2,1)S(1)}, u32[]{:S(2)}, u32[]{:S(2)}) collective-permute-start(bf16[3,128,256]{2,1,0:T(8,128)(2,1)} %get-tuple-element.102), channel_id=1, source_target_pairs={{0,4},{1,5},{2,6},{3,7},{4,0},{5,1},{6,2},{7,3},{8,12},{9,13},{10,... | collective-permute-start | bytes 589832 | tf_op jit(solution)/shard_map/ppermute | solution.py:46
  116.5 1.5 %collective-permute-start.17 = (bf16[3,128,256]{2,1,0:T(8,128)(2,1)}, bf16[3,128,256]{2,1,0:T(8,128)(2,1)S(1)}, u32[]{:S(2)}, u32[]{:S(2)}) collective-permute-start(bf16[3,128,256]{2,1,0:T(8,128)(2,1)} %get-tuple-element.105), channel_id=1, source_target_pairs={{0,3},{1,2},{2,5},{3,4},{4,7},{5,6},{6,1},{7,0},{8,11},{9,10},{10,... | collective-permute-start | bytes 589832 | tf_op jit(solution)/shard_map/ppermute | solution.py:55
  119.1 7.9 %collective-permute-start.18 = (bf16[3,128,256]{2,1,0:T(8,128)(2,1)}, bf16[3,128,256]{2,1,0:T(8,128)(2,1)}, u32[]{:S(2)}, u32[]{:S(2)}) collective-permute-start(bf16[3,128,256]{2,1,0:T(8,128)(2,1)} %get-tuple-element.106), channel_id=1, source_target_pairs={{0,5},{1,4},{2,7},{3,6},{4,1},{5,0},{6,3},{7,2},{8,13},{9,12},{10,... | collective-permute-start | bytes 589832 | tf_op jit(solution)/shard_map/ppermute | solution.py:55
  127.0 2.4 %shard_map.102 = (bf16[128,4096]{1,0:T(8,128)(2,1)}, bf16[128,4096]{1,0:T(8,128)(2,1)}, bf16[128,4096]{1,0:T(8,128)(2,1)}, f32[8,128]{1,0:T(8,128)}) custom-call(bf16[2,3,128,256]{3,2,1,0:T(8,128)(2,1)} %get-tuple-element.81.refs_0_, bf16[2,3,128,256]{3,2,1,0:T(8,128)(2,1)} %copy-done.4, bf16[2,3,128,256]{3,2,1,0:T(8,128)(2,1)} %copy-done.5, ...), custom_call_target="tpu_custom_call" | custom-call | flops 55000000 | bytes 65536 | tf_op jit(solution)/shard_map/pallas_call | solution.py:217
  129.5 4.1 %collective-permute-done.18.refs_6_ = bf16[3,128,256]{2,1,0:T(8,128)(2,1)} collective-permute-done((bf16[3,128,256]{2,1,0:T(8,128)(2,1)}, bf16[3,128,256]{2,1,0:T(8,128)(2,1)}, u32[]{:S(2)}, u32[]{:S(2)}) %collective-permute-start.18) | collective-permute-done | bytes 196640 | tf_op jit(solution)/shard_map/ppermute | solution.py:55
  133.6 2.4 %shard_map.103 = (bf16[128,4096]{1,0:T(8,128)(2,1)}, bf16[128,4096]{1,0:T(8,128)(2,1)}, bf16[128,4096]{1,0:T(8,128)(2,1)}, f32[8,128]{1,0:T(8,128)}) custom-call(bf16[3,128,256]{2,1,0:T(8,128)(2,1)} %get-tuple-element.100.refs_0_, bf16[3,128,256]{2,1,0:T(8,128)(2,1)} %copy-done.8, ...), custom_call_target="tpu_custom_call", output_to_operand_aliasing={{0}: (8, {}), {1}: (9, {}), {2}: (10, {})} | custom-call | flops 55000000 | bytes 65536 | tf_op jit(solution)/shard_map/pallas_call | solution.py:217
  137.1 2.1 %shard_map.104 = (bf16[128,4096]{1,0:T(8,128)(2,1)}, f32[8,128]{1,0:T(8,128)}) custom-call(bf16[2,8,8,2,16,128]{5,4,3,2,1,0:T(8,128)(2,1)} %bitcast.16, f32[8,128]{1,0:T(8,128)} %get-tuple-element.113.refs_0_), custom_call_target="tpu_custom_call" | custom-call | flops 55000000 | bytes 65536 | tf_op jit(solution)/shard_map/pallas_call | solution.py:287
  (73 shorter events, 19.2 us)
Async XLA Ops:
  0.6 24.2 %copy-start.14 = (s32[16]{0:T(128)S(1)}, s32[16]{0:T(128)}, u32[]{:S(2)}) copy-start(s32[16]{0:T(128)} %param.11) | copy-start | bytes 196
  4.6 19.4 %collective-permute-start = (bf16[5,4,128,256]{3,2,1,0:T(8,128)(2,1)}, bf16[5,4,128,256]{3,2,1,0:T(8,128)(2,1)S(1)}, u32[]{:S(2)}, u32[]{:S(2)}) collective-permute-start(bf16[5,4,128,256]{3,2,1,0:T(8,128)(2,1)} %get-tuple-element.61), channel_id=1, source_target_pairs={{0,1},{1,0},{2,3},{3,2},{4,5},{5,4},{6,7},{7,6},{8,9},{9,8},{10,11... | collective-permute-start | bytes 3932168 | tf_op jit(solution)/shard_map/ppermute | solution.py:50
  6.1 9.6 %collective-permute-start.4 = (bf16[4,128,256]{2,1,0:T(8,128)(2,1)}, bf16[4,128,256]{2,1,0:T(8,128)(2,1)S(1)}, u32[]{:S(2)}, u32[]{:S(2)}) collective-permute-start(bf16[4,128,256]{2,1,0:T(8,128)(2,1)} %get-tuple-element.68), channel_id=1, source_target_pairs={{0,2},{1,3},{2,4},{3,5},{4,6},{5,7},{6,0},{7,1},{8,10},{9,11},{10,... | collective-permute-start | bytes 786440 | tf_op jit(solution)/shard_map/ppermute | solution.py:46
  7.5 20.3 %collective-permute-start.5 = (bf16[4,128,256]{2,1,0:T(8,128)(2,1)}, bf16[4,128,256]{2,1,0:T(8,128)(2,1)S(1)}, u32[]{:S(2)}, u32[]{:S(2)}) collective-permute-start(bf16[4,128,256]{2,1,0:T(8,128)(2,1)} %get-tuple-element.69), channel_id=1, source_target_pairs={{0,4},{1,5},{2,6},{3,7},{4,0},{5,1},{6,2},{7,3},{8,12},{9,13},{10,... | collective-permute-start | bytes 786440 | tf_op jit(solution)/shard_map/ppermute | solution.py:46
  10.2 17.7 %collective-permute-start.6 = (bf16[4,128,256]{2,1,0:T(8,128)(2,1)}, bf16[4,128,256]{2,1,0:T(8,128)(2,1)}, u32[]{:S(2)}, u32[]{:S(2)}) collective-permute-start(bf16[4,128,256]{2,1,0:T(8,128)(2,1)} %get-tuple-element.70), channel_id=1, source_target_pairs={{0,6},{1,7},{2,0},{3,1},{4,2},{5,3},{6,4},{7,5},{8,14},{9,15},{10,... | collective-permute-start | bytes 786440 | tf_op jit(solution)/shard_map/ppermute | solution.py:46
  11.2 17.9 %collective-permute-start.7 = (bf16[4,128,256]{2,1,0:T(8,128)(2,1)}, bf16[4,128,256]{2,1,0:T(8,128)(2,1)}, u32[]{:S(2)}, u32[]{:S(2)}) collective-permute-start(bf16[4,128,256]{2,1,0:T(8,128)(2,1)} %get-tuple-element.71), channel_id=1, source_target_pairs={{0,3},{1,2},{2,5},{3,4},{4,7},{5,6},{6,1},{7,0},{8,11},{9,10},{10,... | collective-permute-start | bytes 786440 | tf_op jit(solution)/shard_map/ppermute | solution.py:55
  15.7 18.7 %copy-start.6 = (bf16[4,128,256]{2,1,0:T(8,128)(2,1)}, bf16[4,128,256]{2,1,0:T(8,128)(2,1)S(1)}, u32[]{:S(2)}) copy-start(bf16[4,128,256]{2,1,0:T(8,128)(2,1)S(1)} %collective-permute-done.4.refs_1_) | copy-start | bytes 786436
  15.7 18.7 %collective-permute-start.8 = (bf16[4,128,256]{2,1,0:T(8,128)(2,1)}, bf16[4,128,256]{2,1,0:T(8,128)(2,1)}, u32[]{:S(2)}, u32[]{:S(2)}) collective-permute-start(bf16[4,128,256]{2,1,0:T(8,128)(2,1)} %get-tuple-element.72), channel_id=1, source_target_pairs={{0,5},{1,4},{2,7},{3,6},{4,1},{5,0},{6,3},{7,2},{8,13},{9,12},{10,... | collective-permute-start | bytes 786440 | tf_op jit(solution)/shard_map/ppermute | solution.py:55
  24.1 10.4 %collective-permute-start.9 = (bf16[4,128,256]{2,1,0:T(8,128)(2,1)}, bf16[4,128,256]{2,1,0:T(8,128)(2,1)}, u32[]{:S(2)}, u32[]{:S(2)}) collective-permute-start(bf16[4,128,256]{2,1,0:T(8,128)(2,1)} %get-tuple-element.73), channel_id=1, source_target_pairs={{0,7},{1,6},{2,1},{3,0},{4,3},{5,2},{6,5},{7,4},{8,15},{9,14},{10,... | collective-permute-start | bytes 786440 | tf_op jit(solution)/shard_map/ppermute | solution.py:55
  27.8 33.7 %collective-permute-start.1 = (bf16[2,4,128,256]{3,2,1,0:T(8,128)(2,1)}, bf16[2,4,128,256]{3,2,1,0:T(8,128)(2,1)S(1)}, u32[]{:S(2)}, u32[]{:S(2)}) collective-permute-start(bf16[2,4,128,256]{3,2,1,0:T(8,128)(2,1)} %get-tuple-element.64), channel_id=1, source_target_pairs={{0,2},{1,3},{2,4},{3,5},{4,6},{5,7},{6,0},{7,1},{8,10},{9,11},{10,... | collective-permute-start | bytes 1572872 | tf_op jit(solution)/shard_map/ppermute | solution.py:46
  27.9 35.3 %collective-permute-start.2 = (bf16[2,4,128,256]{3,2,1,0:T(8,128)(2,1)}, bf16[2,4,128,256]{3,2,1,0:T(8,128)(2,1)S(1)}, u32[]{:S(2)}, u32[]{:S(2)}) collective-permute-start(bf16[2,4,128,256]{3,2,1,0:T(8,128)(2,1)} %get-tuple-element.65), channel_id=1, source_target_pairs={{0,4},{1,5},{2,6},{3,7},{4,0},{5,1},{6,2},{7,3},{8,12},{9,13},{10,... | collective-permute-start | bytes 1572872 | tf_op jit(solution)/shard_map/ppermute | solution.py:46
  29.1 34.0 %collective-permute-start.3 = (bf16[2,4,128,256]{3,2,1,0:T(8,128)(2,1)}, bf16[2,4,128,256]{3,2,1,0:T(8,128)(2,1)}, u32[]{:S(2)}, u32[]{:S(2)}) collective-permute-start(bf16[2,4,128,256]{3,2,1,0:T(8,128)(2,1)} %get-tuple-element.66), channel_id=1, source_target_pairs={{0,6},{1,7},{2,0},{3,1},{4,2},{5,3},{6,4},{7,5},{8,14},{9,15},{10,... | collective-permute-start | bytes 1572872 | tf_op jit(solution)/shard_map/ppermute | solution.py:46
  58.1 38.4 %collective-permute-start.10 = (bf16[2,3,128,256]{3,2,1,0:T(8,128)(2,1)}, bf16[2,3,128,256]{3,2,1,0:T(8,128)(2,1)S(1)}, u32[]{:S(2)}, u32[]{:S(2)}) collective-permute-start(bf16[2,3,128,256]{3,2,1,0:T(8,128)(2,1)} %get-tuple-element.82), channel_id=1, source_target_pairs={{0,2},{1,3},{2,4},{3,5},{4,6},{5,7},{6,0},{7,1},{8,10},{9,11},{10,... | collective-permute-start | bytes 1179656 | tf_op jit(solution)/shard_map/ppermute | solution.py:46
  60.7 35.8 %collective-permute-start.11 = (bf16[2,3,128,256]{3,2,1,0:T(8,128)(2,1)}, bf16[2,3,128,256]{3,2,1,0:T(8,128)(2,1)S(1)}, u32[]{:S(2)}, u32[]{:S(2)}) collective-permute-start(bf16[2,3,128,256]{3,2,1,0:T(8,128)(2,1)} %get-tuple-element.83), channel_id=1, source_target_pairs={{0,4},{1,5},{2,6},{3,7},{4,0},{5,1},{6,2},{7,3},{8,12},{9,13},{10,... | collective-permute-start | bytes 1179656 | tf_op jit(solution)/shard_map/ppermute | solution.py:46
  61.6 35.0 %collective-permute-start.12 = (bf16[2,3,128,256]{3,2,1,0:T(8,128)(2,1)}, bf16[2,3,128,256]{3,2,1,0:T(8,128)(2,1)}, u32[]{:S(2)}, u32[]{:S(2)}) collective-permute-start(bf16[2,3,128,256]{3,2,1,0:T(8,128)(2,1)} %get-tuple-element.84), channel_id=1, source_target_pairs={{0,6},{1,7},{2,0},{3,1},{4,2},{5,3},{6,4},{7,5},{8,14},{9,15},{10,... | collective-permute-start | bytes 1179656 | tf_op jit(solution)/shard_map/ppermute | solution.py:46
  74.7 27.7 %all-to-all-start = ((bf16[256,16,128]{2,1,0:T(8,128)(2,1)}), bf16[256,16,128]{2,1,0:T(8,128)(2,1)S(1)}, u32[]{:S(2)}, u32[]{:S(2)}) async-start(bf16[256,16,128]{2,1,0:T(8,128)(2,1)} %bitcast.18), calls=%async_computation | async-start | bytes 2097152 | tf_op jit(solution)/shard_map/all_to_all | solution.py:554
  99.4 27.5 %collective-permute-start.16 = (bf16[5,3,128,256]{3,2,1,0:T(8,128)(2,1)}, bf16[5,3,128,256]{3,2,1,0:T(8,128)(2,1)}, u32[]{:S(2)}, u32[]{:S(2)}) collective-permute-start(bf16[5,3,128,256]{3,2,1,0:T(8,128)(2,1)} %get-tuple-element.104), channel_id=1, source_target_pairs={{0,1},{1,0},{2,3},{3,2},{4,5},{5,4},{6,7},{7,6},{8,9},{9,8},{10,11... | collective-permute-start | bytes 2949128 | tf_op jit(solution)/shard_map/ppermute | solution.py:50
  106.3 29.8 %all-to-all-start.1 = ((bf16[16,1,16,16,128]{4,3,2,1,0:T(8,128)(2,1)}), bf16[16,1,16,16,128]{4,3,2,1,0:T(8,128)(2,1)S(1)}, u32[]{:S(2)}, u32[]{:S(2)}) async-start(bf16[16,1,16,16,128]{4,3,2,1,0:T(8,128)(2,1)} %get-tuple-element.99), calls=%async_computation.1 | async-start | bytes 2097152 | tf_op jit(solution)/shard_map/all_to_all | solution.py:566
  111.4 7.7 %collective-permute-start.13 = (bf16[3,128,256]{2,1,0:T(8,128)(2,1)}, bf16[3,128,256]{2,1,0:T(8,128)(2,1)S(1)}, u32[]{:S(2)}, u32[]{:S(2)}) collective-permute-start(bf16[3,128,256]{2,1,0:T(8,128)(2,1)} %get-tuple-element.101), channel_id=1, source_target_pairs={{0,2},{1,3},{2,4},{3,5},{4,6},{5,7},{6,0},{7,1},{8,10},{9,11},{10,... | collective-permute-start | bytes 589832 | tf_op jit(solution)/shard_map/ppermute | solution.py:46
  112.9 16.5 %collective-permute-start.14 = (bf16[3,128,256]{2,1,0:T(8,128)(2,1)}, bf16[3,128,256]{2,1,0:T(8,128)(2,1)S(1)}, u32[]{:S(2)}, u32[]{:S(2)}) collective-permute-start(bf16[3,128,256]{2,1,0:T(8,128)(2,1)} %get-tuple-element.102), channel_id=1, source_target_pairs={{0,4},{1,5},{2,6},{3,7},{4,0},{5,1},{6,2},{7,3},{8,12},{9,13},{10,... | collective-permute-start | bytes 589832 | tf_op jit(solution)/shard_map/ppermute | solution.py:46
  115.4 14.0 %collective-permute-start.15 = (bf16[3,128,256]{2,1,0:T(8,128)(2,1)}, bf16[3,128,256]{2,1,0:T(8,128)(2,1)S(1)}, u32[]{:S(2)}, u32[]{:S(2)}) collective-permute-start(bf16[3,128,256]{2,1,0:T(8,128)(2,1)} %get-tuple-element.103), channel_id=1, source_target_pairs={{0,6},{1,7},{2,0},{3,1},{4,2},{5,3},{6,4},{7,5},{8,14},{9,15},{10,... | collective-permute-start | bytes 589832 | tf_op jit(solution)/shard_map/ppermute | solution.py:46
  116.5 12.9 %collective-permute-start.17 = (bf16[3,128,256]{2,1,0:T(8,128)(2,1)}, bf16[3,128,256]{2,1,0:T(8,128)(2,1)S(1)}, u32[]{:S(2)}, u32[]{:S(2)}) collective-permute-start(bf16[3,128,256]{2,1,0:T(8,128)(2,1)} %get-tuple-element.105), channel_id=1, source_target_pairs={{0,3},{1,2},{2,5},{3,4},{4,7},{5,6},{6,1},{7,0},{8,11},{9,10},{10,... | collective-permute-start | bytes 589832 | tf_op jit(solution)/shard_map/ppermute | solution.py:55
  119.1 14.5 %collective-permute-start.18 = (bf16[3,128,256]{2,1,0:T(8,128)(2,1)}, bf16[3,128,256]{2,1,0:T(8,128)(2,1)}, u32[]{:S(2)}, u32[]{:S(2)}) collective-permute-start(bf16[3,128,256]{2,1,0:T(8,128)(2,1)} %get-tuple-element.106), channel_id=1, source_target_pairs={{0,5},{1,4},{2,7},{3,6},{4,1},{5,0},{6,3},{7,2},{8,13},{9,12},{10,... | collective-permute-start | bytes 589832 | tf_op jit(solution)/shard_map/ppermute | solution.py:55
  127.0 6.6 %collective-permute-start.19 = (bf16[3,128,256]{2,1,0:T(8,128)(2,1)}, bf16[3,128,256]{2,1,0:T(8,128)(2,1)}, u32[]{:S(2)}, u32[]{:S(2)}) collective-permute-start(bf16[3,128,256]{2,1,0:T(8,128)(2,1)} %get-tuple-element.107), channel_id=1, source_target_pairs={{0,7},{1,6},{2,1},{3,0},{4,3},{5,2},{6,5},{7,4},{8,15},{9,14},{10,... | collective-permute-start | bytes 589832 | tf_op jit(solution)/shard_map/ppermute | solution.py:55
  (13 other events, 52.4 us)
